TPU v7x, 256 devices: a whole 4x4x8 slice. The times are simulated.
256 devices in a mesh: prow: 32 (over x_hi, z, core), pcol: 8 (over y, x_lo).
Axes of the slice: x: 4 (x_hi: 2, x_lo: 2; x = x_hi * 2 + x_lo), y: 4, z: 8, core: 2. Of those that a mesh axis runs over, the one named last changes fastest.
Arguments:
- features: bfloat16 [32768, 256], P(('prow', 'pcol')), may hold values from -6 to 6
- cotangent: bfloat16 [32768, 256], P(('prow', 'pcol')), may hold values from -0.1875 to 0.1875
- self_weight: bfloat16 [256, 256], replicated, may hold values from -0.375 to 0.375
- basis_weights: bfloat16 [32, 256, 256], replicated, may hold values from -0.375 to 0.375
- coefficients: float32 [2690, 32], replicated, may hold values from -1 to 1
- tile_list: int32 [32, 8, 16, 3], P('prow', 'pcol'), may hold values from 0 to 1344, as said below
- tile_mask: int32 [32, 8, 16, 128, 128], P('prow', 'pcol'), may hold values 0 or 1
- live_tiles: int32 [32, 8], P('prow', 'pcol'), may hold values from 1 to 16, as said below
Outputs:
- layer_output: bfloat16 [32768, 256], P(('prow', 'pcol'))
- coefficient_grads: float32 [2690, 32], replicated
Inputs may be any that keep to these rules, and one draw needn't show every extreme that they name: `tile_list`: entries are (relation below 1345, source row index below 32, target column index below 8). `live_tiles`: tile slots at or beyond a cell's count are padding.
All inputs are finite; a program needn't handle non-finite values. No bound on the sum of `tile_mask` on one device may be relied on, other than what follows from the above.
Results may differ from a plain program's by a relative error of at most 0.0054.
Values may be sent and summed in bfloat16 or wider, within the bound.
No kernel may reach another device: no remote copies, remote signals or barrier semaphores. Data moves between devices by JAX's collectives and lax.ppermute only.
A program may use at most 64 MiB of HBM per device.

v0:
```python
import functools
import jax
import jax.numpy as jnp
from jax import lax
from jax.experimental import pallas as pl
from jax.experimental.pallas import tpu as pltpu
from jax.sharding import PartitionSpec as P

F32, BF16 = jnp.float32, jnp.bfloat16
VMEM = pl.BlockSpec(memory_space=pltpu.VMEM)
SMEM = pl.BlockSpec(memory_space=pltpu.SMEM)
ANY = pl.BlockSpec(memory_space=pl.ANY)
HBM = pl.BlockSpec(memory_space=pltpu.HBM)
LANES = 128
DIAGONAL = 16
PAYLOAD = 48


def params(mib):
    return pltpu.CompilerParams(vmem_limit_bytes=mib * 1024 * 1024)


def cost(flops, moved):
    return pl.CostEstimate(flops=flops, bytes_accessed=moved, transcendentals=0)


def split(wide):
    high = wide.astype(BF16)
    return high, (wide - high.astype(F32)).astype(BF16)


def iota(shape, dim):
    return lax.broadcasted_iota(jnp.int32, shape, dim)


def weights_kernel(parts, row_ref, coefficient_ref, basis_ref, weight_ref, spread, basis, weight, in_sems, out_sems):
    bases, named = coefficient_ref.shape
    sides = row_ref.shape[1]
    depth, width = basis.shape[1:]
    size = depth // parts
    tall, wide = sides * DIAGONAL, bases * DIAGONAL
    arrive, leave = [], []
    for part in range(parts):
        rows = pl.ds(part * size, size)
        arrive.append(pltpu.make_async_copy(basis_ref.at[:, rows, :], basis.at[:, rows, :], in_sems.at[part]))
        leave.append(pltpu.make_async_copy(weight.at[:, rows, :], weight_ref.at[:, rows, :], out_sems.at[part]))
    for copy in arrive:
        copy.start()
    chosen = (iota((named, sides), 0) == row_ref[...]).astype(F32).astype(BF16)
    rows = (iota((tall, sides), 0) // DIAGONAL == iota((tall, sides), 1)).astype(F32).astype(BF16)
    columns = (iota((bases, wide), 1) // DIAGONAL == iota((bases, wide), 0)).astype(F32).astype(BF16)
    same = iota((tall, wide), 0) % DIAGONAL == iota((tall, wide), 1) % DIAGONAL
    for index, part in enumerate(split(coefficient_ref[...])):
        picked = jnp.dot(part, chosen, preferred_element_type=F32).astype(BF16)
        tower = lax.dot_general(rows, picked, (((1,), (1,)), ((), ())), preferred_element_type=F32).astype(BF16)
        full = jnp.dot(tower, columns, preferred_element_type=F32)
        spread[index] = jnp.where(same, full, 0.0).astype(BF16)
    for start in range(0, depth, DIAGONAL):
        if start % size == 0:
            arrive[start // size].wait()
        part = basis[:, start : start + DIAGONAL, :].reshape(wide, width)
        total = jnp.dot(spread[0], part, preferred_element_type=F32)
        total += jnp.dot(spread[1], part, preferred_element_type=F32)
        weight[:, start : start + DIAGONAL, :] = total.astype(BF16).reshape(sides, DIAGONAL, width)
        if (start + DIAGONAL) % size == 0:
            leave[start // size].start()
    for copy in leave:
        copy.wait()


def relation_weights(rows_named, coefficients_t, basis, parts=4):
    bases, depth, width = basis.shape
    sides = rows_named.shape[1]
    return pl.pallas_call(
        functools.partial(weights_kernel, parts),
        out_shape=jax.ShapeDtypeStruct((sides, depth, width), BF16),
        in_specs=[VMEM, VMEM, HBM],
        out_specs=HBM,
        scratch_shapes=[
            pltpu.VMEM((2, sides * DIAGONAL, bases * DIAGONAL), BF16),
            pltpu.VMEM(basis.shape, BF16),
            pltpu.VMEM((sides, depth, width), BF16),
            pltpu.SemaphoreType.DMA((parts,)),
            pltpu.SemaphoreType.DMA((parts,)),
        ],
        compiler_params=params(56),
        cost_estimate=cost(4 * 10**9, 2 * basis.size * 2),
        name="relation_weights",
    )(rows_named, coefficients_t, basis)


def normalised(mask, rows, dim):
    over = (((dim,), (0,)), ((), ()))
    summed = lax.dot_general(mask, rows, over, preferred_element_type=F32)
    degree = lax.dot_general(mask, jnp.ones((mask.shape[dim], LANES), BF16), over, preferred_element_type=F32)
    scale = (1.0 / (1.0 + degree)).astype(BF16).astype(F32)
    return (summed * jnp.concatenate([scale] * (rows.shape[1] // LANES), axis=1)).astype(BF16)


def copies_into(target, refs, sems):
    copies, at = [], 0
    for index, ref in enumerate(refs):
        size = ref.shape[0]
        copies.append(pltpu.make_async_copy(ref, target.at[pl.ds(at, size)], sems.at[index]))
        at += size
    for copy in copies:
        copy.start()
    return copies


def block_at(index, size):
    return pl.ds(pl.multiple_of(index * size, size), size)


def inverse_kernel(pieces, entry_ref, live_ref, mask_ref, weights_ref, *refs):
    rows_ref, keep_ref, send_ref, total, row, weight, row_sems, sem = refs[pieces:]
    tiles, block, _ = mask_ref.shape
    arrive = copies_into(row, refs[:pieces], row_sems)
    copy = pltpu.make_async_copy(weights_ref.at[pl.ds(tiles, tiles)], weight, sem)
    copy.start()
    total[...] = jnp.zeros_like(total)
    for part in arrive:
        part.wait()
    for tile in range(tiles):
        rows = row[entry_ref[2, tile], :block, :]
        rows_ref[tile] = normalised(mask_ref[tile].astype(F32).astype(BF16), rows, 0)
    copy.wait()
    for tile in range(tiles):
        weighting = (tile < live_ref[0, 0]).astype(F32)
        message = jnp.dot(rows_ref[tile], weight[tile], preferred_element_type=F32) * weighting
        total[block_at(entry_ref[4, tile], block), :] += message
    half = keep_ref.shape[0]
    keep_ref[...] = total[:half, :]
    send_ref[...] = total[half:, :].astype(BF16)


def inverse_messages(entries, live, mask, row_pieces, weights, row_count):
    tiles, block, _ = mask.shape
    width = row_pieces[0].shape[2]
    half = row_count * block // 2
    columns = sum(piece.shape[0] for piece in row_pieces)
    return pl.pallas_call(
        functools.partial(inverse_kernel, len(row_pieces)),
        out_shape=(
            jax.ShapeDtypeStruct((tiles, block, width), BF16),
            jax.ShapeDtypeStruct((half, width), F32),
            jax.ShapeDtypeStruct((half, width), BF16),
        ),
        in_specs=[SMEM, SMEM, VMEM, HBM] + [ANY] * len(row_pieces),
        out_specs=(VMEM, VMEM, VMEM),
        scratch_shapes=[
            pltpu.VMEM((2 * half, width), F32),
            pltpu.VMEM((columns,) + row_pieces[0].shape[1:], BF16),
            pltpu.VMEM((tiles, width, width), BF16),
            pltpu.SemaphoreType.DMA((len(row_pieces),)),
            pltpu.SemaphoreType.DMA,
        ],
        compiler_params=params(52),
        cost_estimate=cost(10**9, 8 * 10**6),
        name="inverse_messages",
    )(entries, live, mask, weights, *row_pieces)


def forward_kernel(entry_ref, live_ref, rows_ref, weights_ref, keep_ref, *refs):
    send_refs, (total, weight, sem) = refs[:-3], refs[-3:]
    tiles, block, _ = rows_ref.shape
    copy = pltpu.make_async_copy(weights_ref.at[pl.ds(0, tiles)], weight, sem)
    copy.start()
    total[...] = jnp.zeros_like(total)
    copy.wait()
    for tile in range(tiles):
        weighting = (tile < live_ref[0, 0]).astype(F32)
        message = jnp.dot(rows_ref[tile], weight[tile], preferred_element_type=F32) * weighting
        total[entry_ref[5, tile]] += message
    pair = keep_ref.shape[0]
    keep_ref[...] = total[:pair]
    for index, ref in enumerate(send_refs):
        ref[...] = total[pair * (index + 1) : pair * (index + 2)].astype(BF16)


def forward_messages(entries, live, rows, weights):
    tiles, block, width = rows.shape
    shape = (X_LO, block, width)
    return pl.pallas_call(
        forward_kernel,
        out_shape=(jax.ShapeDtypeStruct(shape, F32),) + (jax.ShapeDtypeStruct(shape, BF16),) * (Y - 1),
        in_specs=[SMEM, SMEM, VMEM, HBM],
        out_specs=(VMEM,) * Y,
        scratch_shapes=[
            pltpu.VMEM((Y * X_LO, block, width), F32),
            pltpu.VMEM((tiles, width, width), BF16),
            pltpu.SemaphoreType.DMA,
        ],
        compiler_params=params(56),
        cost_estimate=cost(10**9, 4 * 10**6),
        name="forward_messages",
    )(entries, live, rows, weights)


def gradient_kernel(pieces, row_pieces, entry_ref, live_ref, core_ref, mask_ref, inverse_ref, basis_ref, *refs):
    column_refs, row_refs, refs = refs[:pieces], refs[pieces : pieces + row_pieces], refs[pieces + row_pieces :]
    rows_ref, mine_ref, other_ref, column, row, basis, moments, total, column_sem, row_sem, basis_sem = refs
    tiles, block, _ = mask_ref.shape
    bases, depth, width = basis.shape
    sides = 2 * tiles
    copies = copies_into(column, column_refs, column_sem) + copies_into(row, row_refs, row_sem)
    basis_copy = pltpu.make_async_copy(basis_ref, basis, basis_sem)
    basis_copy.start()
    for copy in copies:
        copy.wait()
    for tile in range(tiles):
        rows = column[entry_ref[1, tile], :block, :]
        rows_ref[tile] = normalised(mask_ref[tile].astype(F32).astype(BF16), rows, 1)
    over = (((0,), (0,)), ((), ()))
    for tile in range(tiles):
        target = row[entry_ref[2, tile], block:, :]
        source = column[entry_ref[1, tile], block:, :]
        moments[tile] = lax.dot_general(rows_ref[tile], target, over, preferred_element_type=F32).astype(BF16)
        moments[tiles + tile] = lax.dot_general(
            inverse_ref[tile], source, over, preferred_element_type=F32
        ).astype(BF16)
    basis_copy.wait()
    tall, wide = bases * DIAGONAL, sides * DIAGONAL
    for start in range(0, depth, DIAGONAL):
        left = basis[:, start : start + DIAGONAL, :].reshape(tall, width)
        right = moments[:, start : start + DIAGONAL, :].reshape(wide, width)
        product = lax.dot_general(left, right, (((1,), (1,)), ((), ())), preferred_element_type=F32)
        if start == 0:
            total[...] = product
        else:
            total[...] += product
    same = iota((tall, wide), 0) % DIAGONAL == iota((tall, wide), 1) % DIAGONAL
    rows = (iota((bases, tall), 1) // DIAGONAL == iota((bases, tall), 0)).astype(BF16)
    columns = (iota((wide, sides), 0) // DIAGONAL == iota((wide, sides), 1)).astype(BF16)
    tower = jnp.zeros((bases, wide), F32)
    for part in split(jnp.where(same, total[...], 0.0)):
        tower += jnp.dot(rows, part, preferred_element_type=F32)
    per_tile = jnp.zeros((bases, sides), F32)
    for part in split(tower):
        per_tile += jnp.dot(part, columns, preferred_element_type=F32)
    live = live_ref[0, 0]
    per_tile = jnp.where(iota((bases, sides), 1) % tiles < live, per_tile, 0.0)
    first = core_ref[0] == 0
    forward, inverse = per_tile[:, :tiles], per_tile[:, tiles:]
    names = iota((PAYLOAD - bases, tiles), 0)
    lane = iota((PAYLOAD - bases, tiles), 1)
    for ref, chosen in ((mine_ref, first), (other_ref, jnp.logical_not(first))):
        ref[:bases, :] = jnp.where(chosen, forward, inverse).astype(BF16)
        named = jnp.zeros((PAYLOAD - bases, tiles), jnp.int32)
        for tile in range(tiles):
            name = entry_ref[0, tile] + jnp.where(chosen, 0, entry_ref[3, tile])
            digits = jnp.where(names == 0, name // LANES, jnp.where(names == 1, name % LANES, 0))
            named = jnp.where(lane == tile, digits, named)
        ref[bases:, :] = named.astype(F32).astype(BF16)


def gradients(entries, live, core, mask, row_pieces, inverse_rows, basis, columns):
    tiles, block, _ = mask.shape
    bases, depth, width = basis.shape
    payload = jax.ShapeDtypeStruct((PAYLOAD, tiles), BF16)

    def room(pieces):
        return pltpu.VMEM((sum(piece.shape[0] for piece in pieces), 2 * block, width), BF16)

    return pl.pallas_call(
        functools.partial(gradient_kernel, len(columns), len(row_pieces)),
        out_shape=(jax.ShapeDtypeStruct((tiles, block, width), BF16), payload, payload),
        in_specs=[SMEM, SMEM, SMEM, VMEM, VMEM, HBM] + [ANY] * (len(columns) + len(row_pieces)),
        out_specs=(VMEM, VMEM, VMEM),
        scratch_shapes=[
            room(columns),
            room(row_pieces),
            pltpu.VMEM(basis.shape, BF16),
            pltpu.VMEM((2 * tiles, depth, width), BF16),
            pltpu.VMEM((bases * DIAGONAL, 2 * tiles * DIAGONAL), F32),
            pltpu.SemaphoreType.DMA((len(columns),)),
            pltpu.SemaphoreType.DMA((len(row_pieces),)),
            pltpu.SemaphoreType.DMA,
        ],
        compiler_params=params(50),
        cost_estimate=cost(4 * 10**9, 12 * 10**6),
        name="gradients",
    )(entries, live, core, mask, inverse_rows, basis, *columns, *row_pieces)


def place_kernel(entry_ref, out_ref, total):
    bases, window = out_ref.shape
    count, _, span = entry_ref.shape
    for index in range(count):
        values = entry_ref[index, :bases, :].astype(F32)
        names = entry_ref[index, bases:, :].astype(F32)
        high, low = names[:1], names[1:2]
        chosen = (iota((LANES, span), 0).astype(F32) == low).astype(F32).astype(BF16)
        spread = [jnp.where(high == part, values, 0.0).astype(BF16) for part in range(window // LANES)]
        product = lax.dot_general(
            jnp.concatenate(spread, axis=0), chosen, (((1,), (1,)), ((), ())), preferred_element_type=F32
        )
        if index == 0:
            total[...] = product
        else:
            total[...] += product
    for part in range(window // LANES):
        out_ref[:, part * LANES : part * LANES + LANES] = total[part * bases : part * bases + bases, :]


def place_rows(entries, bases, window):
    return pl.pallas_call(
        place_kernel,
        out_shape=jax.ShapeDtypeStruct((bases, window), F32),
        in_specs=[VMEM],
        out_specs=VMEM,
        scratch_shapes=[pltpu.VMEM((window // LANES * bases, LANES), F32)],
        compiler_params=params(16),
        cost_estimate=cost(10**9, 10**6),
        name="place_rows",
    )(entries)


def join_kernel(plan, count, *refs):
    sems = refs[-1]
    copies = []
    for output, pieces in enumerate(plan):
        at = 0
        for source, start, size in pieces:
            copies.append(
                pltpu.make_async_copy(
                    refs[source].at[pl.ds(start, size)],
                    refs[count + output].at[pl.ds(at, size)],
                    sems.at[len(copies)],
                )
            )
            at += size
    for copy in copies:
        copy.start()
    for copy in copies:
        copy.wait()


def join(sources, plan):
    shape = sources[0].shape[1:]
    sizes = [sum(size for _, _, size in pieces) for pieces in plan]
    return pl.pallas_call(
        functools.partial(join_kernel, plan, len(sources)),
        out_shape=tuple(jax.ShapeDtypeStruct((size,) + shape, sources[0].dtype) for size in sizes),
        in_specs=[ANY] * len(sources),
        out_specs=tuple(ANY for _ in plan),
        scratch_shapes=[pltpu.SemaphoreType.DMA((sum(len(pieces) for pieces in plan),))],
        compiler_params=params(4),
        cost_estimate=cost(0, 10**6),
        name="join",
    )(*sources)


def finish_kernel(base, core_ref, own_ref, partner_ref, out_ref):
    window = own_ref.shape[1]
    shared = window - base
    last = out_ref.shape[1]
    first = core_ref[0] == 0
    out_ref[:, :base] = jnp.where(first, own_ref[:, :base], partner_ref[:, :base])
    out_ref[:, base:window] = jnp.where(first, own_ref[:, base:], partner_ref[:, base:]) + jnp.where(
        first, partner_ref[:, :shared], own_ref[:, :shared]
    )
    out_ref[:, window:] = jnp.where(
        first, partner_ref[:, shared : last - base], own_ref[:, shared : last - base]
    )


def finish(core, own, partner, base, relations):
    return pl.pallas_call(
        functools.partial(finish_kernel, base),
        out_shape=jax.ShapeDtypeStruct((own.shape[0], 2 * relations), F32),
        in_specs=[SMEM, VMEM, VMEM],
        out_specs=VMEM,
        compiler_params=params(8),
        cost_estimate=cost(0, 10**6),
        name="finish",
    )(core, own, partner)


def pack_kernel(feature_ref, cotangent_ref, own_ref, copies_ref, sems):
    block = feature_ref.shape[0]
    copies = [
        pltpu.make_async_copy(ref, own_ref.at[0, pl.ds(index * block, block), :], sems.at[index])
        for index, ref in enumerate((feature_ref, cotangent_ref))
    ]
    for copy in copies:
        copy.start()
    for copy in copies:
        copy.wait()
    for index in range(copies_ref.shape[0]):
        copies_ref[index] = own_ref[0]


def pack(features, cotangent, count):
    block, width = features.shape
    return pl.pallas_call(
        pack_kernel,
        out_shape=tuple(jax.ShapeDtypeStruct((blocks, 2 * block, width), BF16) for blocks in (1, count)),
        in_specs=[HBM, HBM],
        out_specs=(VMEM, VMEM),
        scratch_shapes=[pltpu.SemaphoreType.DMA((2,))],
        compiler_params=params(60),
        cost_estimate=cost(0, 10**6),
        name="pack",
    )(features, cotangent)


X_HI, RING, CORES = 2, 8, 2
Y, X_LO = 4, 2


def from_row(array, dx=0, dz=0, dk=0):
    pairs = []
    for x in range(X_HI):
        for z in range(RING):
            for k in range(CORES):
                source = ((x ^ dx) * RING + (z + dz) % RING) * CORES + (k ^ dk)
                pairs.append((source, (x * RING + z) * CORES + k))
    return lax.ppermute(array, "prow", pairs)


def from_column(array, dy=0, dx=0):
    pairs = []
    for y in range(Y):
        for x in range(X_LO):
            pairs.append((((y + dy) % Y) * X_LO + (x ^ dx), y * X_LO + x))
    return lax.ppermute(array, "pcol", pairs)


def tie(*arrays):
    return lax.optimization_barrier(arrays)


def coordinates():
    row = lax.axis_index("prow")
    column = lax.axis_index("pcol")
    return row // (RING * CORES), (row // CORES) % RING, row % CORES, column // X_LO, column % X_LO


def column_position(source, x, z, k):
    dx = (source // (RING * CORES)) ^ x
    dz = ((source // CORES) % RING - z) % RING
    dk = (source % CORES) ^ k
    even = dx * 4 + ((dz + 2) % RING) // 2
    odd = 8 + 4 * (dz // 4) + 2 * dx + (dz % 4) // 2
    return dk * 16 + jnp.where(dz % 2 == 0, even, odd)


def ordered(first, own, other, dim):
    return jnp.concatenate([jnp.where(first, own, other), jnp.where(first, other, own)], axis=dim)


def row_groups(apart):
    return [
        [(x * RING + z) * CORES + k for x in range(X_HI) for z in range(first, RING, apart)]
        for first in range(apart)
        for k in range(CORES)
    ]


def gather_gradients(mine, arrived, held, place):
    _, _, k, y, x_lo = place
    entries = ordered(k == 0, mine, arrived, 1)
    entries = ordered(x_lo == 0, entries, from_column(entries, dx=1), 1)
    around = [entries] + [from_column(entries, dy=dy) for dy in range(1, Y)]
    entries = jnp.concatenate(
        [functools.reduce(lambda a, dy: jnp.where(y == (at - dy) % Y, around[dy], a), range(1, Y), around[0]) for at in range(Y)],
        axis=1,
    )
    copies = jnp.broadcast_to(entries[None], (X_HI * RING,) + entries.shape)
    copies, *held = tie(copies, *held)
    gathered = lax.all_to_all(copies, "prow", 0, 0, tiled=True, axis_index_groups=row_groups(1))
    return gathered, held


def on_device(features, cotangent, self_weight, basis_weights, coefficients, tile_list, tile_mask, live_tiles):
    block, width = features.shape
    relations = coefficients.shape[0] // 2
    bases = coefficients.shape[1]
    rows_count = X_HI * RING * CORES
    place = coordinates()
    x, z, k, y, x_lo = place
    mask = tile_mask[0, 0]
    relation, source, target = tile_list[0, 0, :, 0], tile_list[0, 0, :, 1], tile_list[0, 0, :, 2]
    apart = ((source % CORES) ^ k) * (X_HI * RING) + source // CORES
    near = (target // X_LO - y) % Y * X_LO + (target % X_LO ^ x_lo)
    shift = jnp.full_like(relation, relations % LANES)
    entries = jnp.stack([relation, column_position(source, x, z, k), target, shift, apart, near])
    rows_named = jnp.concatenate([relation, relation + relations])[None]

    own, copies = pack(features, cotangent, Y * X_LO)
    ring = [from_row(own, dz=dz) for dz in (4, 2, 6)]
    row_blocks = lax.all_to_all(copies, "pcol", 0, 0, tiled=True)
    (even,) = join([ring[2], own, ring[1], ring[0]], (((0, 0, 1), (1, 0, 1), (2, 0, 1), (3, 0, 1)),))
    across = from_row(even, dx=1)
    even, rows_named = tie(even, rows_named)
    weights = relation_weights(rows_named, coefficients.T, basis_weights)
    row_pieces = [row_blocks]
    inverse_rows, keep, send = inverse_messages(entries, live_tiles, mask, row_pieces, weights, rows_count)
    across, inverse_rows, keep, send = tie(across, inverse_rows, keep, send)
    upward, downward = join([even, across], (((0, 1, 2), (1, 1, 2)), ((0, 0, 2), (1, 0, 2))))
    near = (even, across, from_row(upward, dz=1), from_row(downward, dz=7))
    columns = near + tuple(from_row(piece, dk=1) for piece in near)
    inverse_part = (keep + from_row(send, dk=1).astype(F32)).astype(BF16).reshape(X_HI * RING, block, width)
    *columns, inverse_part = tie(*columns, inverse_part)
    inverse_parts = lax.all_to_all(inverse_part, "prow", 0, 0, tiled=True, axis_index_groups=row_groups(1))
    forward_rows, mine, other = gradients(
        entries, live_tiles, k.reshape(1), mask, row_pieces, inverse_rows, basis_weights, columns
    )
    arrived, forward_rows = tie(from_row(other, dk=1), forward_rows)
    gathered, (forward_rows, inverse_parts) = gather_gradients(mine, arrived, (forward_rows, inverse_parts), place)
    forward_pair, *sends = forward_messages(entries, live_tiles, forward_rows, weights)
    sends = [from_column(part, dy=Y - dy) for dy, part in enumerate(sends, 1)]
    base = relations // LANES * LANES
    window = -(-(2 * relations - base) // LANES) * LANES
    placed = place_rows(gathered, bases, window)
    coefficient_grads = finish(k.reshape(1), placed, from_row(placed, dk=1), base, relations).T
    _, *sends = tie(placed, *sends)
    for part in sends:
        forward_pair += part.astype(F32)
    forward_sum = forward_pair[0] + from_column(forward_pair[1].astype(BF16), dx=1).astype(F32)
    layer_sum = jnp.dot(features, self_weight, preferred_element_type=F32)
    layer_sum += jnp.sum(inverse_parts.astype(F32), axis=0) + forward_sum
    return layer_sum.astype(BF16), coefficient_grads


def solution(mesh):
    return jax.shard_map(
        on_device,
        mesh=mesh,
        in_specs=(
            P(("prow", "pcol"), None),
            P(("prow", "pcol"), None),
            P(),
            P(),
            P(),
            P("prow", "pcol", None, None),
            P("prow", "pcol", None, None, None),
            P("prow", "pcol"),
        ),
        out_specs=(P(("prow", "pcol"), None), P()),
        check_vma=False,
    )
```

profile of v0, /device:TPU:32, one launch (start us, length us, event | category | flops | bytes accessed | tf_op | source)
XLA Modules:
  0.0 126.1 jit_solution(5743463945885995718)
XLA Ops:
  0.7 2.0 %pack.1 = (bf16[1,256,256]{2,1,0:T(8,128)(2,1)}, bf16[8,256,256]{2,1,0:T(8,128)(2,1)}) custom-call(bf16[128,256]{1,0:T(8,128)(2,1)} %feature_ref.1, bf16[128,256]{1,0:T(8,128)(2,1)} %cotangent_ref.1), custom_call_target="tpu_custom_call" | custom-call | bytes 1000000 | tf_op jit(solution)/shard_map/pack/pallas_call | solution.py:396
  2.7 3.3 %collective-permute-start = (bf16[1,256,256]{2,1,0:T(8,128)(2,1)}, bf16[1,256,256]{2,1,0:T(8,128)(2,1)S(1)}, u32[]{:S(2)}, u32[]{:S(2)}) collective-permute-start(bf16[1,256,256]{2,1,0:T(8,128)(2,1)} %get-tuple-element.39.refs_1_), channel_id=1, source_target_pairs={{96,0},{104,8},{112,16},{120,24},{0,32},{8,40},{16,48},{24,56},{32... | collective-permute-start | bytes 393224 | tf_op jit(solution)/shard_map/ppermute | solution.py:419
  6.0 2.2 %collective-permute-start.1 = (bf16[1,256,256]{2,1,0:T(8,128)(2,1)}, bf16[1,256,256]{2,1,0:T(8,128)(2,1)S(1)}, u32[]{:S(2)}, u32[]{:S(2)}) collective-permute-start(bf16[1,256,256]{2,1,0:T(8,128)(2,1)} %get-tuple-element.39.refs_1_), channel_id=1, source_target_pairs={{32,0},{40,8},{48,16},{56,24},{64,32},{72,40},{80,48},{88,56},{96,... | collective-permute-start | bytes 393224 | tf_op jit(solution)/shard_map/ppermute | solution.py:419
  8.3 4.9 %collective-permute-start.2 = (bf16[1,256,256]{2,1,0:T(8,128)(2,1)}, bf16[1,256,256]{2,1,0:T(8,128)(2,1)S(1)}, u32[]{:S(2)}, u32[]{:S(2)}) collective-permute-start(bf16[1,256,256]{2,1,0:T(8,128)(2,1)} %get-tuple-element.39.refs_1_), channel_id=1, source_target_pairs={{64,0},{72,8},{80,16},{88,24},{96,32},{104,40},{112,48},{120,56},{... | collective-permute-start | bytes 393224 | tf_op jit(solution)/shard_map/ppermute | solution.py:419
  13.2 5.4 %all-to-all-start = ((bf16[8,256,256]{2,1,0:T(8,128)(2,1)}), bf16[8,256,256]{2,1,0:T(8,128)(2,1)S(1)}, u32[]{:S(2)}, u32[]{:S(2)}) async-start(bf16[8,256,256]{2,1,0:T(8,128)(2,1)} %get-tuple-element.41), calls=%async_computation | async-start | bytes 2097152 | tf_op jit(solution)/shard_map/all_to_all | solution.py:493
  18.7 5.5 %collective-permute-done.2.refs_3_ = bf16[1,256,256]{2,1,0:T(8,128)(2,1)S(1)} collective-permute-done((bf16[1,256,256]{2,1,0:T(8,128)(2,1)}, bf16[1,256,256]{2,1,0:T(8,128)(2,1)S(1)}, u32[]{:S(2)}, u32[]{:S(2)}) %collective-permute-start.2) | collective-permute-done | bytes 131104 | tf_op jit(solution)/shard_map/ppermute | solution.py:419
  24.9 3.1 %collective-permute-start.3 = (bf16[4,256,256]{2,1,0:T(8,128)(2,1)S(1)}, bf16[4,256,256]{2,1,0:T(8,128)(2,1)S(1)}, u32[]{:S(2)}, u32[]{:S(2)}) collective-permute-start(bf16[4,256,256]{2,1,0:T(8,128)(2,1)S(1)} %join.2.refs_0_), channel_id=1, source_target_pairs={{128,0},{136,8},{144,16},{152,24},{160,32},{168,40},{176,48},{184,... | collective-permute-start | bytes 1572872 | tf_op jit(solution)/shard_map/ppermute | solution.py:419
  29.3 8.4 %relation_weights.1.weights_ref = bf16[32,256,256]{2,1,0:T(8,128)(2,1)} custom-call(s32[1,32]{1,0:T(1,128)} %add_bitcast_fusion.row_ref, f32[32,2690]{1,0:T(8,128)} %bitcast.59, bf16[32,256,256]{2,1,0:T(8,128)(2,1)} %basis_ref.3), custom_call_target="tpu_custom_call" | custom-call | flops 4000000000 | bytes 8388608 | tf_op jit(solution)/shard_map/relation_weights/pallas_call | solution.py:74
  38.7 5.6 %inverse_messages.1 = (bf16[16,128,256]{2,1,0:T(8,128)(2,1)S(1)}, f32[2048,256]{1,0:T(8,128)}, bf16[2048,256]{1,0:T(8,128)(2,1)}) custom-call(s32[6,16]{1,0:T(8,128)S(1)} %stack.2.entry_ref, s32[1,1]{1,0:T(1,128)S(6)} %copy.10.live_ref, s32[16,128,128]{2,1,0:T(8,128)} %bitcast.56, bf16[32,256,256]{2,1,0:T(8,128)(2,1)} %relation_weights.1.weights_ref, ...), custom_call_target="tpu_custom_call" | custom-call | flops 1000000000 | bytes 8000000 | tf_op jit(solution)/shard_map/inverse_messages/pallas_call | solution.py:142
  44.8 1.9 %collective-permute-start.5 = (bf16[4,256,256]{2,1,0:T(8,128)(2,1)S(1)}, bf16[4,256,256]{2,1,0:T(8,128)(2,1)S(1)}, u32[]{:S(2)}, u32[]{:S(2)}) collective-permute-start(bf16[4,256,256]{2,1,0:T(8,128)(2,1)S(1)} %get-tuple-element.49), channel_id=1, source_target_pairs={{112,0},{120,8},{0,16},{8,24},{16,32},{24,40},{32,48},{40,56},{48,... | collective-permute-start | bytes 1572872 | tf_op jit(solution)/shard_map/ppermute | solution.py:419
  47.2 11.8 %collective-permute-done.4.refs_2_ = bf16[4,256,256]{2,1,0:T(8,128)(2,1)S(1)} collective-permute-done((bf16[4,256,256]{2,1,0:T(8,128)(2,1)S(1)}, bf16[4,256,256]{2,1,0:T(8,128)(2,1)S(1)}, u32[]{:S(2)}, u32[]{:S(2)}) %collective-permute-start.4) | collective-permute-done | bytes 524320 | tf_op jit(solution)/shard_map/ppermute | solution.py:419
  59.5 2.9 %add_convert_fusion = bf16[2048,256]{1,0:T(8,128)(2,1)} fusion(f32[2048,256]{1,0:T(8,128)} %get-tuple-element.50, bf16[2048,256]{1,0:T(8,128)(2,1)S(1)} %collective-permute-done.10), kind=kLoop, calls=%fused_computation.1 | loop fusion | flops 1572864 | bytes 4194304 | tf_op jit(solution)/shard_map/convert_element_type | solution.py:504
  64.0 6.3 %all-to-all-start.1 = ((bf16[16,128,256]{2,1,0:T(8,128)(2,1)}), bf16[16,128,256]{2,1,0:T(8,128)(2,1)}, u32[]{:S(2)}, u32[]{:S(2)}) async-start(bf16[16,128,256]{2,1,0:T(8,128)(2,1)} %bitcast.55), calls=%async_computation.1 | async-start | bytes 2097152 | tf_op jit(solution)/shard_map/all_to_all | solution.py:506
  70.3 1.0 copy-done.5
  71.3 8.9 %gradients.1 = (bf16[16,128,256]{2,1,0:T(8,128)(2,1)}, bf16[48,16]{1,0:T(8,128)(2,1)S(1)}, bf16[48,16]{1,0:T(8,128)(2,1)S(1)}) custom-call(s32[6,16]{1,0:T(8,128)S(1)} %stack.2.entry_ref, s32[1,1]{1,0:T(1,128)S(6)} %copy.10.live_ref, s32[1]{0:T(128)} %bitcast.3.core_ref, s32[16,128,128]{2,1,0:T(8,128)} %bitcast.57, bf16[16,128,256]{2,1,0:T(8,128)(2,1)} %copy-done.3, ...), custom_call_target="tpu_custom_call" | custom-call | flops 4000000000 | bytes 12000000 | tf_op jit(solution)/shard_map/gradients/pallas_call | solution.py:265
  80.3 1.2 collective-permute-done.11
  82.5 3.2 %collective-permute-done.12 = bf16[48,32]{1,0:T(8,128)(2,1)S(1)} collective-permute-done((bf16[48,32]{1,0:T(8,128)(2,1)S(1)}, bf16[48,32]{1,0:T(8,128)(2,1)S(1)}, u32[]{:S(2)}, u32[]{:S(2)}) %collective-permute-start.12) | collective-permute-done | bytes 3104 | tf_op jit(solution)/shard_map/ppermute | solution.py:427
  86.8 2.7 %collective-permute-start.14 = (bf16[48,64]{1,0:T(8,128)(2,1)S(1)}, bf16[48,64]{1,0:T(8,128)(2,1)S(1)}, u32[]{:S(2)}, u32[]{:S(2)}) collective-permute-start(bf16[48,64]{1,0:T(8,128)(2,1)S(1)} %pad_maximum_fusion.2), channel_id=1, source_target_pairs={{4,0},{5,1},{6,2},{7,3},{0,4},{1,5},{2,6},{3,7},{12,8},{13,9},{14,... | collective-permute-start | bytes 18440 | tf_op jit(solution)/shard_map/ppermute | solution.py:427
  89.5 1.4 %collective-permute-start.15 = (bf16[48,64]{1,0:T(8,128)(2,1)S(1)}, bf16[48,64]{1,0:T(8,128)(2,1)S(1)}, u32[]{:S(2)}, u32[]{:S(2)}) collective-permute-start(bf16[48,64]{1,0:T(8,128)(2,1)S(1)} %pad_maximum_fusion.2), channel_id=1, source_target_pairs={{2,0},{3,1},{4,2},{5,3},{6,4},{7,5},{0,6},{1,7},{10,8},{11,9},{12,... | collective-permute-start | bytes 18440 | tf_op jit(solution)/shard_map/ppermute | solution.py:427
  90.9 1.1 collective-permute-done.14
  92.0 1.2 collective-permute-done.15
  93.3 5.2 %all-to-all-done.1 = bf16[16,128,256]{2,1,0:T(8,128)(2,1)} async-done(((bf16[16,128,256]{2,1,0:T(8,128)(2,1)}), bf16[16,128,256]{2,1,0:T(8,128)(2,1)}, u32[]{:S(2)}, u32[]{:S(2)}) %all-to-all-start.1) | async-done | bytes 1048608 | tf_op jit(solution)/shard_map/all_to_all | solution.py:506
  99.3 5.6 %all-to-all-start.2 = ((bf16[16,48,256]{2,1,0:T(8,128)(2,1)}), bf16[16,48,256]{2,1,0:T(8,128)(2,1)S(1)}, u32[]{:S(2)}, u32[]{:S(2)}) async-start(bf16[16,48,256]{2,1,0:T(8,128)(2,1)} %broadcast_in_dim.10), calls=%async_computation.2 | async-start | bytes 786432 | tf_op jit(solution)/shard_map/all_to_all | solution.py:472
  104.9 4.2 %forward_messages.1 = (f32[2,128,256]{2,1,0:T(8,128)}, bf16[2,128,256]{2,1,0:T(8,128)(2,1)}, bf16[2,128,256]{2,1,0:T(8,128)(2,1)}, bf16[2,128,256]{2,1,0:T(8,128)(2,1)}) custom-call(s32[6,16]{1,0:T(8,128)} %copy-done.2, s32[1,1]{1,0:T(1,128)S(6)} %copy.10.live_ref, bf16[16,128,256]{2,1,0:T(8,128)(2,1)} %get-tuple-element.67.rows_ref, ...), custom_call_target="tpu_custom_call" | custom-call | flops 1000000000 | bytes 4000000 | tf_op jit(solution)/shard_map/forward_messages/pallas_call | solution.py:184
  109.1 1.0 collective-permute-start.16
  110.1 2.7 %collective-permute-start.17 = (bf16[2,128,256]{2,1,0:T(8,128)(2,1)}, bf16[2,128,256]{2,1,0:T(8,128)(2,1)S(1)}, u32[]{:S(2)}, u32[]{:S(2)}) collective-permute-start(bf16[2,128,256]{2,1,0:T(8,128)(2,1)} %get-tuple-element.71), channel_id=1, source_target_pairs={{4,0},{5,1},{6,2},{7,3},{0,4},{1,5},{2,6},{3,7},{12,8},{13,9},{14,... | collective-permute-start | bytes 393224 | tf_op jit(solution)/shard_map/ppermute | solution.py:427
  112.8 1.4 %collective-permute-start.18 = (bf16[2,128,256]{2,1,0:T(8,128)(2,1)}, bf16[2,128,256]{2,1,0:T(8,128)(2,1)S(1)}, u32[]{:S(2)}, u32[]{:S(2)}) collective-permute-start(bf16[2,128,256]{2,1,0:T(8,128)(2,1)} %get-tuple-element.72), channel_id=1, source_target_pairs={{2,0},{3,1},{4,2},{5,3},{6,4},{7,5},{0,6},{1,7},{10,8},{11,9},{12,... | collective-permute-start | bytes 393224 | tf_op jit(solution)/shard_map/ppermute | solution.py:427
  114.2 4.9 %all-to-all-done.2.entry_ref = bf16[16,48,256]{2,1,0:T(8,128)(2,1)S(1)} async-done(((bf16[16,48,256]{2,1,0:T(8,128)(2,1)}), bf16[16,48,256]{2,1,0:T(8,128)(2,1)S(1)}, u32[]{:S(2)}, u32[]{:S(2)}) %all-to-all-start.2) | async-done | bytes 393248 | tf_op jit(solution)/shard_map/all_to_all | solution.py:472
  119.0 1.0 place_rows.1.own_ref
  120.2 1.0 collective-permute-start.19
  121.1 1.4 %convert_reduce_fusion = f32[128,256]{1,0:T(8,128)S(1)} fusion(bf16[16,128,256]{2,1,0:T(8,128)(2,1)} %all-to-all-done.1), kind=kLoop, calls=%fused_computation | loop fusion | flops 1015808 | bytes 1179648 | tf_op jit(solution)/shard_map/reduce_sum | solution.py:523
  122.6 1.9 %collective-permute-done.19 = bf16[128,256]{1,0:T(8,128)(2,1)S(1)} collective-permute-done((bf16[128,256]{1,0:T(8,128)(2,1)S(1)}, bf16[128,256]{1,0:T(8,128)(2,1)S(1)}, u32[]{:S(2)}, u32[]{:S(2)}) %collective-permute-start.19) | collective-permute-done | bytes 65568 | tf_op jit(solution)/shard_map/ppermute | solution.py:427
  (66 shorter events, 10.2 us)
Async XLA Ops:
  0.6 123.9 %copy-start = (bf16[256,256]{1,0:T(8,128)(2,1)S(1)}, bf16[256,256]{1,0:T(8,128)(2,1)}, u32[]{:S(2)}) copy-start(bf16[256,256]{1,0:T(8,128)(2,1)} %param.10) | copy-start | bytes 393220
  0.6 17.9 %copy-start.9 = (s32[1,1,16,3]{2,1,3,0:T(1,128)S(1)}, s32[1,1,16,3]{2,1,3,0:T(1,128)}, u32[]{:S(2)}) copy-start(s32[1,1,16,3]{2,1,3,0:T(1,128)} %param.13) | copy-start | bytes 580
  2.7 21.5 %copy-start.1 = (bf16[1,256,256]{2,1,0:T(8,128)(2,1)S(1)}, bf16[1,256,256]{2,1,0:T(8,128)(2,1)}, u32[]{:S(2)}) copy-start(bf16[1,256,256]{2,1,0:T(8,128)(2,1)} %get-tuple-element.39.refs_1_) | copy-start | bytes 393220
  2.7 16.0 %collective-permute-start = (bf16[1,256,256]{2,1,0:T(8,128)(2,1)}, bf16[1,256,256]{2,1,0:T(8,128)(2,1)S(1)}, u32[]{:S(2)}, u32[]{:S(2)}) collective-permute-start(bf16[1,256,256]{2,1,0:T(8,128)(2,1)} %get-tuple-element.39.refs_1_), channel_id=1, source_target_pairs={{96,0},{104,8},{112,16},{120,24},{0,32},{8,40},{16,48},{24,56},{32... | collective-permute-start | bytes 393224 | tf_op jit(solution)/shard_map/ppermute | solution.py:419
  6.0 12.7 %collective-permute-start.1 = (bf16[1,256,256]{2,1,0:T(8,128)(2,1)}, bf16[1,256,256]{2,1,0:T(8,128)(2,1)S(1)}, u32[]{:S(2)}, u32[]{:S(2)}) collective-permute-start(bf16[1,256,256]{2,1,0:T(8,128)(2,1)} %get-tuple-element.39.refs_1_), channel_id=1, source_target_pairs={{32,0},{40,8},{48,16},{56,24},{64,32},{72,40},{80,48},{88,56},{96,... | collective-permute-start | bytes 393224 | tf_op jit(solution)/shard_map/ppermute | solution.py:419
  8.3 15.9 %collective-permute-start.2 = (bf16[1,256,256]{2,1,0:T(8,128)(2,1)}, bf16[1,256,256]{2,1,0:T(8,128)(2,1)S(1)}, u32[]{:S(2)}, u32[]{:S(2)}) collective-permute-start(bf16[1,256,256]{2,1,0:T(8,128)(2,1)} %get-tuple-element.39.refs_1_), channel_id=1, source_target_pairs={{64,0},{72,8},{80,16},{88,24},{96,32},{104,40},{112,48},{120,56},{... | collective-permute-start | bytes 393224 | tf_op jit(solution)/shard_map/ppermute | solution.py:419
  13.2 24.5 %all-to-all-start = ((bf16[8,256,256]{2,1,0:T(8,128)(2,1)}), bf16[8,256,256]{2,1,0:T(8,128)(2,1)S(1)}, u32[]{:S(2)}, u32[]{:S(2)}) async-start(bf16[8,256,256]{2,1,0:T(8,128)(2,1)} %get-tuple-element.41), calls=%async_computation | async-start | bytes 2097152 | tf_op jit(solution)/shard_map/all_to_all | solution.py:493
  24.9 19.4 %collective-permute-start.3 = (bf16[4,256,256]{2,1,0:T(8,128)(2,1)S(1)}, bf16[4,256,256]{2,1,0:T(8,128)(2,1)S(1)}, u32[]{:S(2)}, u32[]{:S(2)}) collective-permute-start(bf16[4,256,256]{2,1,0:T(8,128)(2,1)S(1)} %join.2.refs_0_), channel_id=1, source_target_pairs={{128,0},{136,8},{144,16},{152,24},{160,32},{168,40},{176,48},{184,... | collective-permute-start | bytes 1572872 | tf_op jit(solution)/shard_map/ppermute | solution.py:419
  29.3 41.0 %copy-start.2 = (s32[6,16]{1,0:T(8,128)}, s32[6,16]{1,0:T(8,128)S(1)}, u32[]{:S(2)}) copy-start(s32[6,16]{1,0:T(8,128)S(1)} %stack.2.entry_ref) | copy-start | bytes 1156
  44.3 18.0 %copy-start.3 = (bf16[16,128,256]{2,1,0:T(8,128)(2,1)}, bf16[16,128,256]{2,1,0:T(8,128)(2,1)S(1)}, u32[]{:S(2)}) copy-start(bf16[16,128,256]{2,1,0:T(8,128)(2,1)S(1)} %get-tuple-element.45.inverse_ref) | copy-start | bytes 3145732
  44.3 15.1 %collective-permute-start.10 = (bf16[2048,256]{1,0:T(8,128)(2,1)}, bf16[2048,256]{1,0:T(8,128)(2,1)S(1)}, u32[]{:S(2)}, u32[]{:S(2)}) collective-permute-start(bf16[2048,256]{1,0:T(8,128)(2,1)} %get-tuple-element.51), channel_id=1, source_target_pairs={{8,0},{0,8},{24,16},{16,24},{40,32},{32,40},{56,48},{48,56},{72,64... | collective-permute-start | bytes 3145736 | tf_op jit(solution)/shard_map/ppermute | solution.py:419
  44.6 14.4 %collective-permute-start.4 = (bf16[4,256,256]{2,1,0:T(8,128)(2,1)S(1)}, bf16[4,256,256]{2,1,0:T(8,128)(2,1)S(1)}, u32[]{:S(2)}, u32[]{:S(2)}) collective-permute-start(bf16[4,256,256]{2,1,0:T(8,128)(2,1)S(1)} %get-tuple-element.48), channel_id=1, source_target_pairs={{16,0},{24,8},{32,16},{40,24},{48,32},{56,40},{64,48},{72,56},{80,... | collective-permute-start | bytes 1572872 | tf_op jit(solution)/shard_map/ppermute | solution.py:419
  44.8 14.3 %collective-permute-start.5 = (bf16[4,256,256]{2,1,0:T(8,128)(2,1)S(1)}, bf16[4,256,256]{2,1,0:T(8,128)(2,1)S(1)}, u32[]{:S(2)}, u32[]{:S(2)}) collective-permute-start(bf16[4,256,256]{2,1,0:T(8,128)(2,1)S(1)} %get-tuple-element.49), channel_id=1, source_target_pairs={{112,0},{120,8},{0,16},{8,24},{16,32},{24,40},{32,48},{40,56},{48,... | collective-permute-start | bytes 1572872 | tf_op jit(solution)/shard_map/ppermute | solution.py:419
  46.7 15.7 %collective-permute-start.6 = (bf16[4,256,256]{2,1,0:T(8,128)(2,1)S(1)}, bf16[4,256,256]{2,1,0:T(8,128)(2,1)S(1)}, u32[]{:S(2)}, u32[]{:S(2)}) collective-permute-start(bf16[4,256,256]{2,1,0:T(8,128)(2,1)S(1)} %join.2.refs_0_), channel_id=1, source_target_pairs={{8,0},{0,8},{24,16},{16,24},{40,32},{32,40},{56,48},{48,56},{72,64... | collective-permute-start | bytes 1572872 | tf_op jit(solution)/shard_map/ppermute | solution.py:419
  46.7 15.7 %collective-permute-start.7 = (bf16[4,256,256]{2,1,0:T(8,128)(2,1)S(1)}, bf16[4,256,256]{2,1,0:T(8,128)(2,1)S(1)}, u32[]{:S(2)}, u32[]{:S(2)}) collective-permute-start(bf16[4,256,256]{2,1,0:T(8,128)(2,1)S(1)} %collective-permute-done.3.refs_1_), channel_id=1, source_target_pairs={{8,0},{0,8},{24,16},{16,24},{40,32},{32,40},{56,48},{48,56},{72,64... | collective-permute-start | bytes 1572872 | tf_op jit(solution)/shard_map/ppermute | solution.py:419
  59.0 3.4 %collective-permute-start.8 = (bf16[4,256,256]{2,1,0:T(8,128)(2,1)S(1)}, bf16[4,256,256]{2,1,0:T(8,128)(2,1)S(1)}, u32[]{:S(2)}, u32[]{:S(2)}) collective-permute-start(bf16[4,256,256]{2,1,0:T(8,128)(2,1)S(1)} %collective-permute-done.4.refs_2_), channel_id=1, source_target_pairs={{8,0},{0,8},{24,16},{16,24},{40,32},{32,40},{56,48},{48,56},{72,64... | collective-permute-start | bytes 1572872 | tf_op jit(solution)/shard_map/ppermute | solution.py:419
  59.1 4.1 %collective-permute-start.9 = (bf16[4,256,256]{2,1,0:T(8,128)(2,1)S(1)}, bf16[4,256,256]{2,1,0:T(8,128)(2,1)S(1)}, u32[]{:S(2)}, u32[]{:S(2)}) collective-permute-start(bf16[4,256,256]{2,1,0:T(8,128)(2,1)S(1)} %collective-permute-done.5.refs_3_), channel_id=1, source_target_pairs={{8,0},{0,8},{24,16},{16,24},{40,32},{32,40},{56,48},{48,56},{72,64... | collective-permute-start | bytes 1572872 | tf_op jit(solution)/shard_map/ppermute | solution.py:419
  64.0 34.6 %all-to-all-start.1 = ((bf16[16,128,256]{2,1,0:T(8,128)(2,1)}), bf16[16,128,256]{2,1,0:T(8,128)(2,1)}, u32[]{:S(2)}, u32[]{:S(2)}) async-start(bf16[16,128,256]{2,1,0:T(8,128)(2,1)} %bitcast.55), calls=%async_computation.1 | async-start | bytes 2097152 | tf_op jit(solution)/shard_map/all_to_all | solution.py:506
  70.3 1.0 copy-start.5
  80.2 1.3 %collective-permute-start.11 = (bf16[48,16]{1,0:T(8,128)(2,1)S(1)}, bf16[48,16]{1,0:T(8,128)(2,1)S(1)}, u32[]{:S(2)}, u32[]{:S(2)}) collective-permute-start(bf16[48,16]{1,0:T(8,128)(2,1)S(1)} %get-tuple-element.61), channel_id=1, source_target_pairs={{8,0},{0,8},{24,16},{16,24},{40,32},{32,40},{56,48},{48,56},{72,64... | collective-permute-start | bytes 4616 | tf_op jit(solution)/shard_map/ppermute | solution.py:419
  81.6 4.2 %collective-permute-start.12 = (bf16[48,32]{1,0:T(8,128)(2,1)S(1)}, bf16[48,32]{1,0:T(8,128)(2,1)S(1)}, u32[]{:S(2)}, u32[]{:S(2)}) collective-permute-start(bf16[48,32]{1,0:T(8,128)(2,1)S(1)} %pad_maximum_fusion.1), channel_id=1, source_target_pairs={{1,0},{0,1},{3,2},{2,3},{5,4},{4,5},{7,6},{6,7},{9,8},{8,9},{11,10... | collective-permute-start | bytes 9224 | tf_op jit(solution)/shard_map/ppermute | solution.py:427
  85.9 5.0 %collective-permute-start.13 = (bf16[48,64]{1,0:T(8,128)(2,1)S(1)}, bf16[48,64]{1,0:T(8,128)(2,1)S(1)}, u32[]{:S(2)}, u32[]{:S(2)}) collective-permute-start(bf16[48,64]{1,0:T(8,128)(2,1)S(1)} %pad_maximum_fusion.2), channel_id=1, source_target_pairs={{6,0},{7,1},{0,2},{1,3},{2,4},{3,5},{4,6},{5,7},{14,8},{15,9},{8,1... | collective-permute-start | bytes 18440 | tf_op jit(solution)/shard_map/ppermute | solution.py:427
  86.8 5.2 %collective-permute-start.14 = (bf16[48,64]{1,0:T(8,128)(2,1)S(1)}, bf16[48,64]{1,0:T(8,128)(2,1)S(1)}, u32[]{:S(2)}, u32[]{:S(2)}) collective-permute-start(bf16[48,64]{1,0:T(8,128)(2,1)S(1)} %pad_maximum_fusion.2), channel_id=1, source_target_pairs={{4,0},{5,1},{6,2},{7,3},{0,4},{1,5},{2,6},{3,7},{12,8},{13,9},{14,... | collective-permute-start | bytes 18440 | tf_op jit(solution)/shard_map/ppermute | solution.py:427
  89.5 3.7 %collective-permute-start.15 = (bf16[48,64]{1,0:T(8,128)(2,1)S(1)}, bf16[48,64]{1,0:T(8,128)(2,1)S(1)}, u32[]{:S(2)}, u32[]{:S(2)}) collective-permute-start(bf16[48,64]{1,0:T(8,128)(2,1)S(1)} %pad_maximum_fusion.2), channel_id=1, source_target_pairs={{2,0},{3,1},{4,2},{5,3},{6,4},{7,5},{0,6},{1,7},{10,8},{11,9},{12,... | collective-permute-start | bytes 18440 | tf_op jit(solution)/shard_map/ppermute | solution.py:427
  99.3 19.7 %all-to-all-start.2 = ((bf16[16,48,256]{2,1,0:T(8,128)(2,1)}), bf16[16,48,256]{2,1,0:T(8,128)(2,1)S(1)}, u32[]{:S(2)}, u32[]{:S(2)}) async-start(bf16[16,48,256]{2,1,0:T(8,128)(2,1)} %broadcast_in_dim.10), calls=%async_computation.2 | async-start | bytes 786432 | tf_op jit(solution)/shard_map/all_to_all | solution.py:472
  109.1 11.0 %copy-start.7 = (f32[2,128,256]{2,1,0:T(8,128)S(1)}, f32[2,128,256]{2,1,0:T(8,128)}, u32[]{:S(2)}) copy-start(f32[2,128,256]{2,1,0:T(8,128)} %get-tuple-element.68) | copy-start | bytes 786436
  109.1 11.0 %collective-permute-start.16 = (bf16[2,128,256]{2,1,0:T(8,128)(2,1)}, bf16[2,128,256]{2,1,0:T(8,128)(2,1)S(1)}, u32[]{:S(2)}, u32[]{:S(2)}) collective-permute-start(bf16[2,128,256]{2,1,0:T(8,128)(2,1)} %get-tuple-element.70), channel_id=1, source_target_pairs={{6,0},{7,1},{0,2},{1,3},{2,4},{3,5},{4,6},{5,7},{14,8},{15,9},{8,1... | collective-permute-start | bytes 393224 | tf_op jit(solution)/shard_map/ppermute | solution.py:427
  110.1 9.9 %collective-permute-start.17 = (bf16[2,128,256]{2,1,0:T(8,128)(2,1)}, bf16[2,128,256]{2,1,0:T(8,128)(2,1)S(1)}, u32[]{:S(2)}, u32[]{:S(2)}) collective-permute-start(bf16[2,128,256]{2,1,0:T(8,128)(2,1)} %get-tuple-element.71), channel_id=1, source_target_pairs={{4,0},{5,1},{6,2},{7,3},{0,4},{1,5},{2,6},{3,7},{12,8},{13,9},{14,... | collective-permute-start | bytes 393224 | tf_op jit(solution)/shard_map/ppermute | solution.py:427
  112.8 11.7 %copy-start.8 = (bf16[128,256]{1,0:T(8,128)(2,1)S(1)}, bf16[128,256]{1,0:T(8,128)(2,1)}, u32[]{:S(2)}) copy-start(bf16[128,256]{1,0:T(8,128)(2,1)} %feature_ref.1) | copy-start | bytes 196612
  112.8 7.3 %collective-permute-start.18 = (bf16[2,128,256]{2,1,0:T(8,128)(2,1)}, bf16[2,128,256]{2,1,0:T(8,128)(2,1)S(1)}, u32[]{:S(2)}, u32[]{:S(2)}) collective-permute-start(bf16[2,128,256]{2,1,0:T(8,128)(2,1)} %get-tuple-element.72), channel_id=1, source_target_pairs={{2,0},{3,1},{4,2},{5,3},{6,4},{7,5},{0,6},{1,7},{10,8},{11,9},{12,... | collective-permute-start | bytes 393224 | tf_op jit(solution)/shard_map/ppermute | solution.py:427
  120.2 4.4 %collective-permute-start.19 = (bf16[128,256]{1,0:T(8,128)(2,1)S(1)}, bf16[128,256]{1,0:T(8,128)(2,1)S(1)}, u32[]{:S(2)}, u32[]{:S(2)}) collective-permute-start(bf16[128,256]{1,0:T(8,128)(2,1)S(1)} %fusion.4), channel_id=1, source_target_pairs={{1,0},{0,1},{3,2},{2,3},{5,4},{4,5},{7,6},{6,7},{9,8},{8,9},{11,10... | collective-permute-start | bytes 196616 | tf_op jit(solution)/shard_map/ppermute | solution.py:427
  122.5 2.8 %collective-permute-start.20 = (f32[32,1536]{1,0:T(8,128)S(1)}, f32[32,1536]{1,0:T(8,128)S(1)}, u32[]{:S(2)}, u32[]{:S(2)}) collective-permute-start(f32[32,1536]{1,0:T(8,128)S(1)} %place_rows.1.own_ref), channel_id=1, source_target_pairs={{8,0},{0,8},{24,16},{16,24},{40,32},{32,40},{56,48},{48,56},{72,64... | collective-permute-start | bytes 589832 | tf_op jit(solution)/shard_map/ppermute | solution.py:419
  (3 other events, 2.6 us)
where the time goes:
time: 127 us; the launch traced here: 126 us
  starting transfers between devices  46.2 us (36%)
  waiting for transfers between devices  36.1 us (28%)
  Pallas kernels  31.6 us (25%)
  other arithmetic  5.28 us (4%)
  local copies, waits for them, and re-layouts  4.46 us (4%)
  between operations  1.63 us (1%)
    ppermute x13, waiting for transfers between devices, from_row(): return lax.ppermute(array, 'prow', pairs)  18.5 us
    ppermute x13, starting transfers between devices, from_row(): return lax.ppermute(array, 'prow', pairs)  16.9 us
    ppermute x8, starting transfers between devices, from_column(): return lax.ppermute(array, 'pcol', pairs)  12 us
    pallas_call x1, Pallas kernels, gradients(): pl.pallas_call(functools.partial(gradient_kernel, len(columns), len(row_p...  8.88 us
    pallas_call x1, Pallas kernels, relation_weights(): pl.pallas_call(functools.partial(weights_kernel, parts), out_shape=jax.Sh...  8.41 us
    ppermute x8, waiting for transfers between devices, from_column(): return lax.ppermute(array, 'pcol', pairs)  7.44 us
    all_to_all x1, starting transfers between devices, on_device(): lax.all_to_all(inverse_part, 'prow', 0, 0, tiled=True, axis_index_groups=...  6.31 us
    pallas_call x1, Pallas kernels, inverse_messages(): pl.pallas_call(functools.partial(inverse_kernel, len(row_pieces)), out_sh...  5.61 us
  transfers between devices with their start and end apart: 24, of which 10 were waited for; matrix products, arithmetic and copies ran while one was open for 5% of the time, Pallas kernels for 23%

commit v1 on v0

--- a/solution.py
+++ b/solution.py
@@ -499,10 +499,11 @@
     inverse_rows, keep, send = inverse_messages(entries, live_tiles, mask, row_pieces, weights, rows_count)
     across, inverse_rows, keep, send = tie(across, inverse_rows, keep, send)
     upward, downward = join([even, across], (((0, 1, 2), (1, 1, 2)), ((0, 0, 2), (1, 0, 2))))
-    near = (even, across, from_row(upward, dz=1), from_row(downward, dz=7))
-    columns = near + tuple(from_row(piece, dk=1) for piece in near)
+    up, down = from_row(upward, dz=1), from_row(downward, dz=7)
+    swapped = [from_row(even, dk=1), from_row(across, dk=1)]
     inverse_part = (keep + from_row(send, dk=1).astype(F32)).astype(BF16).reshape(X_HI * RING, block, width)
-    *columns, inverse_part = tie(*columns, inverse_part)
+    up, down, inverse_part, *swapped = tie(up, down, inverse_part, *swapped)
+    columns = [even, across, up, down, *swapped, from_row(up, dk=1), from_row(down, dk=1)]
     inverse_parts = lax.all_to_all(inverse_part, "prow", 0, 0, tiled=True, axis_index_groups=row_groups(1))
     forward_rows, mine, other = gradients(
         entries, live_tiles, k.reshape(1), mask, row_pieces, inverse_rows, basis_weights, columns

time: 127 us -> 123 us (0.969)
  local copies, waits for them, and re-layouts: 4.46 us -> 1.9 us
  waiting for transfers between devices: 36.1 us -> 34.6 us
    ppermute x8, starting transfers between devices: 12 us -> 9.38 us  [from_column(): return lax.ppermute(array, 'pcol', pairs)]
    unnamed x22 -> x18, local copies, waits for them, and re-layouts: 3.64 us -> 1.07 us
    all_to_all x1, starting transfers between devices: 5.57 us -> 8 us  [gather_gradients(): lax.all_to_all(copies, 'prow', 0, 0, tiled=True, axis_index_groups=row_gr...]
    all_to_all x1, waiting for transfers between devices: 5.25 us -> 3.12 us  [on_device(): lax.all_to_all(inverse_part, 'prow', 0, 0, tiled=True, axis_index_groups=...]
    ppermute x8, waiting for transfers between devices: 7.44 us -> 8.85 us  [from_column(): return lax.ppermute(array, 'pcol', pairs)]
  transfers between devices with their start and end apart: 24 -> 24, of which waited for: 10 -> 13; matrix products, arithmetic and copies ran while one was open for 5% -> 5% of each run, Pallas kernels for 23% -> 23%
where the time goes in v1:
time: 123 us
  starting transfers between devices  46.9 us (38%)
  waiting for transfers between devices  34.6 us (28%)
  Pallas kernels  31.5 us (26%)
  other arithmetic  5.31 us (4%)
  local copies, waits for them, and re-layouts  1.9 us (2%)
  between operations  1.6 us (1%)
    ppermute x13, waiting for transfers between devices, from_row(): return lax.ppermute(array, 'prow', pairs)  18 us
    ppermute x13, starting transfers between devices, from_row(): return lax.ppermute(array, 'prow', pairs)  17.2 us
    ppermute x8, starting transfers between devices, from_column(): return lax.ppermute(array, 'pcol', pairs)  9.38 us
    pallas_call x1, Pallas kernels, gradients(): pl.pallas_call(functools.partial(gradient_kernel, len(columns), len(row_p...  8.89 us
    ppermute x8, waiting for transfers between devices, from_column(): return lax.ppermute(array, 'pcol', pairs)  8.85 us
    pallas_call x1, Pallas kernels, relation_weights(): pl.pallas_call(functools.partial(weights_kernel, parts), out_shape=jax.Sh...  8.34 us
    all_to_all x1, starting transfers between devices, gather_gradients(): lax.all_to_all(copies, 'prow', 0, 0, tiled=True, axis_index_groups=row_gr...  8 us
    all_to_all x1, starting transfers between devices, on_device(): lax.all_to_all(inverse_part, 'prow', 0, 0, tiled=True, axis_index_groups=...  6.89 us
  transfers between devices with their start and end apart: 24, of which 13 were waited for; matrix products, arithmetic and copies ran while one was open for 5% of the time, Pallas kernels for 23%

profile of v1, /device:TPU:32, one launch (start us, length us, event | category | flops | bytes accessed | tf_op | source)
XLA Modules:
  0.0 122.6 jit_solution(2350328005030214260)
XLA Ops:
  0.7 2.0 %pack.1 = (bf16[1,256,256]{2,1,0:T(8,128)(2,1)}, bf16[8,256,256]{2,1,0:T(8,128)(2,1)}) custom-call(bf16[128,256]{1,0:T(8,128)(2,1)} %feature_ref.1, bf16[128,256]{1,0:T(8,128)(2,1)} %cotangent_ref.1), custom_call_target="tpu_custom_call" | custom-call | bytes 1000000 | tf_op jit(solution)/shard_map/pack/pallas_call | solution.py:396
  2.7 3.3 %collective-permute-start = (bf16[1,256,256]{2,1,0:T(8,128)(2,1)}, bf16[1,256,256]{2,1,0:T(8,128)(2,1)S(1)}, u32[]{:S(2)}, u32[]{:S(2)}) collective-permute-start(bf16[1,256,256]{2,1,0:T(8,128)(2,1)} %get-tuple-element.35.refs_1_), channel_id=1, source_target_pairs={{96,0},{104,8},{112,16},{120,24},{0,32},{8,40},{16,48},{24,56},{32... | collective-permute-start | bytes 393224 | tf_op jit(solution)/shard_map/ppermute | solution.py:419
  6.0 2.2 %collective-permute-start.1 = (bf16[1,256,256]{2,1,0:T(8,128)(2,1)}, bf16[1,256,256]{2,1,0:T(8,128)(2,1)S(1)}, u32[]{:S(2)}, u32[]{:S(2)}) collective-permute-start(bf16[1,256,256]{2,1,0:T(8,128)(2,1)} %get-tuple-element.35.refs_1_), channel_id=1, source_target_pairs={{32,0},{40,8},{48,16},{56,24},{64,32},{72,40},{80,48},{88,56},{96,... | collective-permute-start | bytes 393224 | tf_op jit(solution)/shard_map/ppermute | solution.py:419
  8.2 4.9 %collective-permute-start.2 = (bf16[1,256,256]{2,1,0:T(8,128)(2,1)}, bf16[1,256,256]{2,1,0:T(8,128)(2,1)S(1)}, u32[]{:S(2)}, u32[]{:S(2)}) collective-permute-start(bf16[1,256,256]{2,1,0:T(8,128)(2,1)} %get-tuple-element.35.refs_1_), channel_id=1, source_target_pairs={{64,0},{72,8},{80,16},{88,24},{96,32},{104,40},{112,48},{120,56},{... | collective-permute-start | bytes 393224 | tf_op jit(solution)/shard_map/ppermute | solution.py:419
  13.2 5.4 %all-to-all-start = ((bf16[8,256,256]{2,1,0:T(8,128)(2,1)}), bf16[8,256,256]{2,1,0:T(8,128)(2,1)S(1)}, u32[]{:S(2)}, u32[]{:S(2)}) async-start(bf16[8,256,256]{2,1,0:T(8,128)(2,1)} %get-tuple-element.37), calls=%async_computation | async-start | bytes 2097152 | tf_op jit(solution)/shard_map/all_to_all | solution.py:493
  18.7 5.5 %collective-permute-done.2.refs_3_ = bf16[1,256,256]{2,1,0:T(8,128)(2,1)S(1)} collective-permute-done((bf16[1,256,256]{2,1,0:T(8,128)(2,1)}, bf16[1,256,256]{2,1,0:T(8,128)(2,1)S(1)}, u32[]{:S(2)}, u32[]{:S(2)}) %collective-permute-start.2) | collective-permute-done | bytes 131104 | tf_op jit(solution)/shard_map/ppermute | solution.py:419
  24.9 3.1 %collective-permute-start.3 = (bf16[4,256,256]{2,1,0:T(8,128)(2,1)S(1)}, bf16[4,256,256]{2,1,0:T(8,128)(2,1)S(1)}, u32[]{:S(2)}, u32[]{:S(2)}) collective-permute-start(bf16[4,256,256]{2,1,0:T(8,128)(2,1)S(1)} %join.2.refs_0_), channel_id=1, source_target_pairs={{128,0},{136,8},{144,16},{152,24},{160,32},{168,40},{176,48},{184,... | collective-permute-start | bytes 1572872 | tf_op jit(solution)/shard_map/ppermute | solution.py:419
  29.3 8.3 %relation_weights.1.weights_ref = bf16[32,256,256]{2,1,0:T(8,128)(2,1)} custom-call(s32[1,32]{1,0:T(1,128)} %add_bitcast_fusion.row_ref, f32[32,2690]{1,0:T(8,128)} %bitcast.59, bf16[32,256,256]{2,1,0:T(8,128)(2,1)} %basis_ref.3), custom_call_target="tpu_custom_call" | custom-call | flops 4000000000 | bytes 8388608 | tf_op jit(solution)/shard_map/relation_weights/pallas_call | solution.py:74
  37.7 1.0 copy-done.4
  38.6 5.6 %inverse_messages.1 = (bf16[16,128,256]{2,1,0:T(8,128)(2,1)S(1)}, f32[2048,256]{1,0:T(8,128)}, bf16[2048,256]{1,0:T(8,128)(2,1)}) custom-call(s32[6,16]{1,0:T(8,128)S(1)} %stack.2.entry_ref, s32[1,1]{1,0:T(1,128)S(6)} %copy.10.live_ref, s32[16,128,128]{2,1,0:T(8,128)} %bitcast.56, bf16[32,256,256]{2,1,0:T(8,128)(2,1)} %relation_weights.1.weights_ref, ...), custom_call_target="tpu_custom_call" | custom-call | flops 1000000000 | bytes 8000000 | tf_op jit(solution)/shard_map/inverse_messages/pallas_call | solution.py:142
  45.4 1.8 %collective-permute-start.5 = (bf16[4,256,256]{2,1,0:T(8,128)(2,1)S(1)}, bf16[4,256,256]{2,1,0:T(8,128)(2,1)S(1)}, u32[]{:S(2)}, u32[]{:S(2)}) collective-permute-start(bf16[4,256,256]{2,1,0:T(8,128)(2,1)S(1)} %get-tuple-element.45), channel_id=1, source_target_pairs={{112,0},{120,8},{0,16},{8,24},{16,32},{24,40},{32,48},{40,56},{48,... | collective-permute-start | bytes 1572872 | tf_op jit(solution)/shard_map/ppermute | solution.py:419
  47.7 2.9 %add_convert_fusion = bf16[2048,256]{1,0:T(8,128)(2,1)} fusion(f32[2048,256]{1,0:T(8,128)} %get-tuple-element.46, bf16[2048,256]{1,0:T(8,128)(2,1)S(1)} %collective-permute-done.6), kind=kLoop, calls=%fused_computation.1 | loop fusion | flops 1572864 | bytes 4194304 | tf_op jit(solution)/shard_map/convert_element_type | solution.py:504
  50.6 8.8 %collective-permute-done.4.refs_2_ = bf16[4,256,256]{2,1,0:T(8,128)(2,1)S(1)} collective-permute-done((bf16[4,256,256]{2,1,0:T(8,128)(2,1)S(1)}, bf16[4,256,256]{2,1,0:T(8,128)(2,1)S(1)}, u32[]{:S(2)}, u32[]{:S(2)}) %collective-permute-start.4) | collective-permute-done | bytes 524320 | tf_op jit(solution)/shard_map/ppermute | solution.py:419
  59.4 6.9 %all-to-all-start.1 = ((bf16[16,128,256]{2,1,0:T(8,128)(2,1)}), bf16[16,128,256]{2,1,0:T(8,128)(2,1)}, u32[]{:S(2)}, u32[]{:S(2)}) async-start(bf16[16,128,256]{2,1,0:T(8,128)(2,1)} %bitcast.55), calls=%async_computation.1 | async-start | bytes 2097152 | tf_op jit(solution)/shard_map/all_to_all | solution.py:507
  66.8 1.4 %collective-permute-done.10.refs_7_ = bf16[4,256,256]{2,1,0:T(8,128)(2,1)S(1)} collective-permute-done((bf16[4,256,256]{2,1,0:T(8,128)(2,1)S(1)}, bf16[4,256,256]{2,1,0:T(8,128)(2,1)S(1)}, u32[]{:S(2)}, u32[]{:S(2)}) %collective-permute-start.10) | collective-permute-done | bytes 524320 | tf_op jit(solution)/shard_map/ppermute | solution.py:419
  69.0 8.9 %gradients.1 = (bf16[16,128,256]{2,1,0:T(8,128)(2,1)}, bf16[48,16]{1,0:T(8,128)(2,1)S(1)}, bf16[48,16]{1,0:T(8,128)(2,1)S(1)}) custom-call(s32[6,16]{1,0:T(8,128)S(1)} %stack.2.entry_ref, s32[1,1]{1,0:T(1,128)S(6)} %copy.10.live_ref, s32[1]{0:T(128)} %bitcast.3.core_ref, s32[16,128,128]{2,1,0:T(8,128)} %bitcast.57, bf16[16,128,256]{2,1,0:T(8,128)(2,1)} %copy-done.3, ...), custom_call_target="tpu_custom_call" | custom-call | flops 4000000000 | bytes 12000000 | tf_op jit(solution)/shard_map/gradients/pallas_call | solution.py:265
  78.1 1.0 collective-permute-done.11
  79.3 0.9 collective-permute-start.12
  80.2 3.9 %collective-permute-done.12 = bf16[48,32]{1,0:T(8,128)(2,1)S(1)} collective-permute-done((bf16[48,32]{1,0:T(8,128)(2,1)S(1)}, bf16[48,32]{1,0:T(8,128)(2,1)S(1)}, u32[]{:S(2)}, u32[]{:S(2)}) %collective-permute-start.12) | collective-permute-done | bytes 3104 | tf_op jit(solution)/shard_map/ppermute | solution.py:427
  84.3 2.5 %collective-permute-start.14 = (bf16[48,64]{1,0:T(8,128)(2,1)S(1)}, bf16[48,64]{1,0:T(8,128)(2,1)S(1)}, u32[]{:S(2)}, u32[]{:S(2)}) collective-permute-start(bf16[48,64]{1,0:T(8,128)(2,1)S(1)} %pad_maximum_fusion.2), channel_id=1, source_target_pairs={{4,0},{5,1},{6,2},{7,3},{0,4},{1,5},{2,6},{3,7},{12,8},{13,9},{14,... | collective-permute-start | bytes 18440 | tf_op jit(solution)/shard_map/ppermute | solution.py:427
  86.9 1.4 %collective-permute-start.15 = (bf16[48,64]{1,0:T(8,128)(2,1)S(1)}, bf16[48,64]{1,0:T(8,128)(2,1)S(1)}, u32[]{:S(2)}, u32[]{:S(2)}) collective-permute-start(bf16[48,64]{1,0:T(8,128)(2,1)S(1)} %pad_maximum_fusion.2), channel_id=1, source_target_pairs={{2,0},{3,1},{4,2},{5,3},{6,4},{7,5},{0,6},{1,7},{10,8},{11,9},{12,... | collective-permute-start | bytes 18440 | tf_op jit(solution)/shard_map/ppermute | solution.py:427
  88.3 0.9 collective-permute-done.13
  89.6 0.9 collective-permute-done.15
  90.7 3.1 %all-to-all-done.1 = bf16[16,128,256]{2,1,0:T(8,128)(2,1)} async-done(((bf16[16,128,256]{2,1,0:T(8,128)(2,1)}), bf16[16,128,256]{2,1,0:T(8,128)(2,1)}, u32[]{:S(2)}, u32[]{:S(2)}) %all-to-all-start.1) | async-done | bytes 1048608 | tf_op jit(solution)/shard_map/all_to_all | solution.py:507
  94.6 8.0 %all-to-all-start.2 = ((bf16[16,48,256]{2,1,0:T(8,128)(2,1)}), bf16[16,48,256]{2,1,0:T(8,128)(2,1)S(1)}, u32[]{:S(2)}, u32[]{:S(2)}) async-start(bf16[16,48,256]{2,1,0:T(8,128)(2,1)} %broadcast_in_dim.10), calls=%async_computation.2 | async-start | bytes 786432 | tf_op jit(solution)/shard_map/all_to_all | solution.py:472
  102.6 4.2 %forward_messages.1 = (f32[2,128,256]{2,1,0:T(8,128)}, bf16[2,128,256]{2,1,0:T(8,128)(2,1)}, bf16[2,128,256]{2,1,0:T(8,128)(2,1)}, bf16[2,128,256]{2,1,0:T(8,128)(2,1)}) custom-call(s32[6,16]{1,0:T(8,128)} %copy-done.2, s32[1,1]{1,0:T(1,128)S(6)} %copy.10.live_ref, bf16[16,128,256]{2,1,0:T(8,128)(2,1)} %get-tuple-element.59.rows_ref, ...), custom_call_target="tpu_custom_call" | custom-call | flops 1000000000 | bytes 4000000 | tf_op jit(solution)/shard_map/forward_messages/pallas_call | solution.py:184
  107.2 3.8 %collective-permute-start.17 = (bf16[2,128,256]{2,1,0:T(8,128)(2,1)}, bf16[2,128,256]{2,1,0:T(8,128)(2,1)S(1)}, u32[]{:S(2)}, u32[]{:S(2)}) collective-permute-start(bf16[2,128,256]{2,1,0:T(8,128)(2,1)} %get-tuple-element.63), channel_id=1, source_target_pairs={{4,0},{5,1},{6,2},{7,3},{0,4},{1,5},{2,6},{3,7},{12,8},{13,9},{14,... | collective-permute-start | bytes 393224 | tf_op jit(solution)/shard_map/ppermute | solution.py:427
  111.0 4.6 %all-to-all-done.2.entry_ref = bf16[16,48,256]{2,1,0:T(8,128)(2,1)S(1)} async-done(((bf16[16,48,256]{2,1,0:T(8,128)(2,1)}), bf16[16,48,256]{2,1,0:T(8,128)(2,1)S(1)}, u32[]{:S(2)}, u32[]{:S(2)}) %all-to-all-start.2) | async-done | bytes 393248 | tf_op jit(solution)/shard_map/all_to_all | solution.py:472
  115.6 1.0 place_rows.1.own_ref
  116.9 1.4 %convert_reduce_fusion = f32[128,256]{1,0:T(8,128)S(1)} fusion(bf16[16,128,256]{2,1,0:T(8,128)(2,1)} %all-to-all-done.1), kind=kLoop, calls=%fused_computation | loop fusion | flops 1015808 | bytes 1179648 | tf_op jit(solution)/shard_map/reduce_sum | solution.py:524
  118.4 2.6 %collective-permute-done.19 = bf16[128,256]{1,0:T(8,128)(2,1)S(1)} collective-permute-done((bf16[128,256]{1,0:T(8,128)(2,1)S(1)}, bf16[128,256]{1,0:T(8,128)(2,1)S(1)}, u32[]{:S(2)}, u32[]{:S(2)}) %collective-permute-start.19) | collective-permute-done | bytes 65568 | tf_op jit(solution)/shard_map/ppermute | solution.py:427
  121.0 0.8 fusion.3
  (62 shorter events, 7.7 us)
Async XLA Ops:
  0.6 120.4 %copy-start = (bf16[256,256]{1,0:T(8,128)(2,1)S(1)}, bf16[256,256]{1,0:T(8,128)(2,1)}, u32[]{:S(2)}) copy-start(bf16[256,256]{1,0:T(8,128)(2,1)} %param.10) | copy-start | bytes 393220
  0.6 17.9 %copy-start.7 = (s32[1,1,16,3]{2,1,3,0:T(1,128)S(1)}, s32[1,1,16,3]{2,1,3,0:T(1,128)}, u32[]{:S(2)}) copy-start(s32[1,1,16,3]{2,1,3,0:T(1,128)} %param.13) | copy-start | bytes 580
  2.7 21.5 %copy-start.1 = (bf16[1,256,256]{2,1,0:T(8,128)(2,1)S(1)}, bf16[1,256,256]{2,1,0:T(8,128)(2,1)}, u32[]{:S(2)}) copy-start(bf16[1,256,256]{2,1,0:T(8,128)(2,1)} %get-tuple-element.35.refs_1_) | copy-start | bytes 393220
  2.7 16.0 %collective-permute-start = (bf16[1,256,256]{2,1,0:T(8,128)(2,1)}, bf16[1,256,256]{2,1,0:T(8,128)(2,1)S(1)}, u32[]{:S(2)}, u32[]{:S(2)}) collective-permute-start(bf16[1,256,256]{2,1,0:T(8,128)(2,1)} %get-tuple-element.35.refs_1_), channel_id=1, source_target_pairs={{96,0},{104,8},{112,16},{120,24},{0,32},{8,40},{16,48},{24,56},{32... | collective-permute-start | bytes 393224 | tf_op jit(solution)/shard_map/ppermute | solution.py:419
  6.0 12.7 %collective-permute-start.1 = (bf16[1,256,256]{2,1,0:T(8,128)(2,1)}, bf16[1,256,256]{2,1,0:T(8,128)(2,1)S(1)}, u32[]{:S(2)}, u32[]{:S(2)}) collective-permute-start(bf16[1,256,256]{2,1,0:T(8,128)(2,1)} %get-tuple-element.35.refs_1_), channel_id=1, source_target_pairs={{32,0},{40,8},{48,16},{56,24},{64,32},{72,40},{80,48},{88,56},{96,... | collective-permute-start | bytes 393224 | tf_op jit(solution)/shard_map/ppermute | solution.py:419
  8.2 15.9 %collective-permute-start.2 = (bf16[1,256,256]{2,1,0:T(8,128)(2,1)}, bf16[1,256,256]{2,1,0:T(8,128)(2,1)S(1)}, u32[]{:S(2)}, u32[]{:S(2)}) collective-permute-start(bf16[1,256,256]{2,1,0:T(8,128)(2,1)} %get-tuple-element.35.refs_1_), channel_id=1, source_target_pairs={{64,0},{72,8},{80,16},{88,24},{96,32},{104,40},{112,48},{120,56},{... | collective-permute-start | bytes 393224 | tf_op jit(solution)/shard_map/ppermute | solution.py:419
  13.2 24.5 %all-to-all-start = ((bf16[8,256,256]{2,1,0:T(8,128)(2,1)}), bf16[8,256,256]{2,1,0:T(8,128)(2,1)S(1)}, u32[]{:S(2)}, u32[]{:S(2)}) async-start(bf16[8,256,256]{2,1,0:T(8,128)(2,1)} %get-tuple-element.37), calls=%async_computation | async-start | bytes 2097152 | tf_op jit(solution)/shard_map/all_to_all | solution.py:493
  24.9 19.3 %collective-permute-start.3 = (bf16[4,256,256]{2,1,0:T(8,128)(2,1)S(1)}, bf16[4,256,256]{2,1,0:T(8,128)(2,1)S(1)}, u32[]{:S(2)}, u32[]{:S(2)}) collective-permute-start(bf16[4,256,256]{2,1,0:T(8,128)(2,1)S(1)} %join.2.refs_0_), channel_id=1, source_target_pairs={{128,0},{136,8},{144,16},{152,24},{160,32},{168,40},{176,48},{184,... | collective-permute-start | bytes 1572872 | tf_op jit(solution)/shard_map/ppermute | solution.py:419
  29.3 39.7 %copy-start.2 = (s32[6,16]{1,0:T(8,128)}, s32[6,16]{1,0:T(8,128)S(1)}, u32[]{:S(2)}) copy-start(s32[6,16]{1,0:T(8,128)S(1)} %stack.2.entry_ref) | copy-start | bytes 1156
  37.6 1.0 copy-start.4
  44.2 6.4 %copy-start.3 = (bf16[16,128,256]{2,1,0:T(8,128)(2,1)}, bf16[16,128,256]{2,1,0:T(8,128)(2,1)S(1)}, u32[]{:S(2)}) copy-start(bf16[16,128,256]{2,1,0:T(8,128)(2,1)S(1)} %get-tuple-element.41.inverse_ref) | copy-start | bytes 3145732
  44.2 3.5 %collective-permute-start.6 = (bf16[2048,256]{1,0:T(8,128)(2,1)}, bf16[2048,256]{1,0:T(8,128)(2,1)S(1)}, u32[]{:S(2)}, u32[]{:S(2)}) collective-permute-start(bf16[2048,256]{1,0:T(8,128)(2,1)} %get-tuple-element.47), channel_id=1, source_target_pairs={{8,0},{0,8},{24,16},{16,24},{40,32},{32,40},{56,48},{48,56},{72,64... | collective-permute-start | bytes 3145736 | tf_op jit(solution)/shard_map/ppermute | solution.py:419
  44.3 6.2 %collective-permute-start.7 = (bf16[4,256,256]{2,1,0:T(8,128)(2,1)S(1)}, bf16[4,256,256]{2,1,0:T(8,128)(2,1)S(1)}, u32[]{:S(2)}, u32[]{:S(2)}) collective-permute-start(bf16[4,256,256]{2,1,0:T(8,128)(2,1)S(1)} %join.2.refs_0_), channel_id=1, source_target_pairs={{8,0},{0,8},{24,16},{16,24},{40,32},{32,40},{56,48},{48,56},{72,64... | collective-permute-start | bytes 1572872 | tf_op jit(solution)/shard_map/ppermute | solution.py:419
  45.0 14.5 %collective-permute-start.8 = (bf16[4,256,256]{2,1,0:T(8,128)(2,1)S(1)}, bf16[4,256,256]{2,1,0:T(8,128)(2,1)S(1)}, u32[]{:S(2)}, u32[]{:S(2)}) collective-permute-start(bf16[4,256,256]{2,1,0:T(8,128)(2,1)S(1)} %collective-permute-done.3.refs_1_), channel_id=1, source_target_pairs={{8,0},{0,8},{24,16},{16,24},{40,32},{32,40},{56,48},{48,56},{72,64... | collective-permute-start | bytes 1572872 | tf_op jit(solution)/shard_map/ppermute | solution.py:419
  45.2 14.3 %collective-permute-start.4 = (bf16[4,256,256]{2,1,0:T(8,128)(2,1)S(1)}, bf16[4,256,256]{2,1,0:T(8,128)(2,1)S(1)}, u32[]{:S(2)}, u32[]{:S(2)}) collective-permute-start(bf16[4,256,256]{2,1,0:T(8,128)(2,1)S(1)} %get-tuple-element.44), channel_id=1, source_target_pairs={{16,0},{24,8},{32,16},{40,24},{48,32},{56,40},{64,48},{72,56},{80,... | collective-permute-start | bytes 1572872 | tf_op jit(solution)/shard_map/ppermute | solution.py:419
  45.4 14.0 %collective-permute-start.5 = (bf16[4,256,256]{2,1,0:T(8,128)(2,1)S(1)}, bf16[4,256,256]{2,1,0:T(8,128)(2,1)S(1)}, u32[]{:S(2)}, u32[]{:S(2)}) collective-permute-start(bf16[4,256,256]{2,1,0:T(8,128)(2,1)S(1)} %get-tuple-element.45), channel_id=1, source_target_pairs={{112,0},{120,8},{0,16},{8,24},{16,32},{24,40},{32,48},{40,56},{48,... | collective-permute-start | bytes 1572872 | tf_op jit(solution)/shard_map/ppermute | solution.py:419
  59.4 34.4 %all-to-all-start.1 = ((bf16[16,128,256]{2,1,0:T(8,128)(2,1)}), bf16[16,128,256]{2,1,0:T(8,128)(2,1)}, u32[]{:S(2)}, u32[]{:S(2)}) async-start(bf16[16,128,256]{2,1,0:T(8,128)(2,1)} %bitcast.55), calls=%async_computation.1 | async-start | bytes 2097152 | tf_op jit(solution)/shard_map/all_to_all | solution.py:507
  66.3 1.9 %collective-permute-start.10 = (bf16[4,256,256]{2,1,0:T(8,128)(2,1)S(1)}, bf16[4,256,256]{2,1,0:T(8,128)(2,1)S(1)}, u32[]{:S(2)}, u32[]{:S(2)}) collective-permute-start(bf16[4,256,256]{2,1,0:T(8,128)(2,1)S(1)} %collective-permute-done.5.refs_3_), channel_id=1, source_target_pairs={{8,0},{0,8},{24,16},{16,24},{40,32},{32,40},{56,48},{48,56},{72,64... | collective-permute-start | bytes 1572872 | tf_op jit(solution)/shard_map/ppermute | solution.py:419
  66.3 2.7 %collective-permute-start.9 = (bf16[4,256,256]{2,1,0:T(8,128)(2,1)S(1)}, bf16[4,256,256]{2,1,0:T(8,128)(2,1)S(1)}, u32[]{:S(2)}, u32[]{:S(2)}) collective-permute-start(bf16[4,256,256]{2,1,0:T(8,128)(2,1)S(1)} %collective-permute-done.4.refs_2_), channel_id=1, source_target_pairs={{8,0},{0,8},{24,16},{16,24},{40,32},{32,40},{56,48},{48,56},{72,64... | collective-permute-start | bytes 1572872 | tf_op jit(solution)/shard_map/ppermute | solution.py:419
  77.9 1.3 %collective-permute-start.11 = (bf16[48,16]{1,0:T(8,128)(2,1)S(1)}, bf16[48,16]{1,0:T(8,128)(2,1)S(1)}, u32[]{:S(2)}, u32[]{:S(2)}) collective-permute-start(bf16[48,16]{1,0:T(8,128)(2,1)S(1)} %get-tuple-element.53), channel_id=1, source_target_pairs={{8,0},{0,8},{24,16},{16,24},{40,32},{32,40},{56,48},{48,56},{72,64... | collective-permute-start | bytes 4616 | tf_op jit(solution)/shard_map/ppermute | solution.py:419
  79.3 4.9 %collective-permute-start.12 = (bf16[48,32]{1,0:T(8,128)(2,1)S(1)}, bf16[48,32]{1,0:T(8,128)(2,1)S(1)}, u32[]{:S(2)}, u32[]{:S(2)}) collective-permute-start(bf16[48,32]{1,0:T(8,128)(2,1)S(1)} %pad_maximum_fusion.1), channel_id=1, source_target_pairs={{1,0},{0,1},{3,2},{2,3},{5,4},{4,5},{7,6},{6,7},{9,8},{8,9},{11,10... | collective-permute-start | bytes 9224 | tf_op jit(solution)/shard_map/ppermute | solution.py:427
  84.3 4.9 %collective-permute-start.13 = (bf16[48,64]{1,0:T(8,128)(2,1)S(1)}, bf16[48,64]{1,0:T(8,128)(2,1)S(1)}, u32[]{:S(2)}, u32[]{:S(2)}) collective-permute-start(bf16[48,64]{1,0:T(8,128)(2,1)S(1)} %pad_maximum_fusion.2), channel_id=1, source_target_pairs={{6,0},{7,1},{0,2},{1,3},{2,4},{3,5},{4,6},{5,7},{14,8},{15,9},{8,1... | collective-permute-start | bytes 18440 | tf_op jit(solution)/shard_map/ppermute | solution.py:427
  84.3 5.3 %collective-permute-start.14 = (bf16[48,64]{1,0:T(8,128)(2,1)S(1)}, bf16[48,64]{1,0:T(8,128)(2,1)S(1)}, u32[]{:S(2)}, u32[]{:S(2)}) collective-permute-start(bf16[48,64]{1,0:T(8,128)(2,1)S(1)} %pad_maximum_fusion.2), channel_id=1, source_target_pairs={{4,0},{5,1},{6,2},{7,3},{0,4},{1,5},{2,6},{3,7},{12,8},{13,9},{14,... | collective-permute-start | bytes 18440 | tf_op jit(solution)/shard_map/ppermute | solution.py:427
  86.9 3.7 %collective-permute-start.15 = (bf16[48,64]{1,0:T(8,128)(2,1)S(1)}, bf16[48,64]{1,0:T(8,128)(2,1)S(1)}, u32[]{:S(2)}, u32[]{:S(2)}) collective-permute-start(bf16[48,64]{1,0:T(8,128)(2,1)S(1)} %pad_maximum_fusion.2), channel_id=1, source_target_pairs={{2,0},{3,1},{4,2},{5,3},{6,4},{7,5},{0,6},{1,7},{10,8},{11,9},{12,... | collective-permute-start | bytes 18440 | tf_op jit(solution)/shard_map/ppermute | solution.py:427
  94.6 21.0 %all-to-all-start.2 = ((bf16[16,48,256]{2,1,0:T(8,128)(2,1)}), bf16[16,48,256]{2,1,0:T(8,128)(2,1)S(1)}, u32[]{:S(2)}, u32[]{:S(2)}) async-start(bf16[16,48,256]{2,1,0:T(8,128)(2,1)} %broadcast_in_dim.10), calls=%async_computation.2 | async-start | bytes 786432 | tf_op jit(solution)/shard_map/all_to_all | solution.py:472
  106.7 9.8 %copy-start.5 = (f32[2,128,256]{2,1,0:T(8,128)S(1)}, f32[2,128,256]{2,1,0:T(8,128)}, u32[]{:S(2)}) copy-start(f32[2,128,256]{2,1,0:T(8,128)} %get-tuple-element.60) | copy-start | bytes 786436
  106.7 9.8 %collective-permute-start.16 = (bf16[2,128,256]{2,1,0:T(8,128)(2,1)}, bf16[2,128,256]{2,1,0:T(8,128)(2,1)S(1)}, u32[]{:S(2)}, u32[]{:S(2)}) collective-permute-start(bf16[2,128,256]{2,1,0:T(8,128)(2,1)} %get-tuple-element.62), channel_id=1, source_target_pairs={{6,0},{7,1},{0,2},{1,3},{2,4},{3,5},{4,6},{5,7},{14,8},{15,9},{8,1... | collective-permute-start | bytes 393224 | tf_op jit(solution)/shard_map/ppermute | solution.py:427
  107.2 9.4 %collective-permute-start.17 = (bf16[2,128,256]{2,1,0:T(8,128)(2,1)}, bf16[2,128,256]{2,1,0:T(8,128)(2,1)S(1)}, u32[]{:S(2)}, u32[]{:S(2)}) collective-permute-start(bf16[2,128,256]{2,1,0:T(8,128)(2,1)} %get-tuple-element.63), channel_id=1, source_target_pairs={{4,0},{5,1},{6,2},{7,3},{0,4},{1,5},{2,6},{3,7},{12,8},{13,9},{14,... | collective-permute-start | bytes 393224 | tf_op jit(solution)/shard_map/ppermute | solution.py:427
  111.0 10.0 %copy-start.6 = (bf16[128,256]{1,0:T(8,128)(2,1)S(1)}, bf16[128,256]{1,0:T(8,128)(2,1)}, u32[]{:S(2)}) copy-start(bf16[128,256]{1,0:T(8,128)(2,1)} %feature_ref.1) | copy-start | bytes 196612
  111.0 5.6 %collective-permute-start.18 = (bf16[2,128,256]{2,1,0:T(8,128)(2,1)}, bf16[2,128,256]{2,1,0:T(8,128)(2,1)S(1)}, u32[]{:S(2)}, u32[]{:S(2)}) collective-permute-start(bf16[2,128,256]{2,1,0:T(8,128)(2,1)} %get-tuple-element.64), channel_id=1, source_target_pairs={{2,0},{3,1},{4,2},{5,3},{6,4},{7,5},{0,6},{1,7},{10,8},{11,9},{12,... | collective-permute-start | bytes 393224 | tf_op jit(solution)/shard_map/ppermute | solution.py:427
  116.7 4.4 %collective-permute-start.19 = (bf16[128,256]{1,0:T(8,128)(2,1)S(1)}, bf16[128,256]{1,0:T(8,128)(2,1)S(1)}, u32[]{:S(2)}, u32[]{:S(2)}) collective-permute-start(bf16[128,256]{1,0:T(8,128)(2,1)S(1)} %fusion.4), channel_id=1, source_target_pairs={{1,0},{0,1},{3,2},{2,3},{5,4},{4,5},{7,6},{6,7},{9,8},{8,9},{11,10... | collective-permute-start | bytes 196616 | tf_op jit(solution)/shard_map/ppermute | solution.py:427
  118.3 3.6 %collective-permute-start.20 = (f32[32,1536]{1,0:T(8,128)S(1)}, f32[32,1536]{1,0:T(8,128)S(1)}, u32[]{:S(2)}, u32[]{:S(2)}) collective-permute-start(f32[32,1536]{1,0:T(8,128)S(1)} %place_rows.1.own_ref), channel_id=1, source_target_pairs={{8,0},{0,8},{24,16},{16,24},{40,32},{32,40},{56,48},{48,56},{72,64... | collective-permute-start | bytes 589832 | tf_op jit(solution)/shard_map/ppermute | solution.py:419
  (1 other events, 0.8 us)

commit v2 on v1

--- a/solution.py
+++ b/solution.py
@@ -509,8 +509,8 @@
         entries, live_tiles, k.reshape(1), mask, row_pieces, inverse_rows, basis_weights, columns
     )
     arrived, forward_rows = tie(from_row(other, dk=1), forward_rows)
-    gathered, (forward_rows, inverse_parts) = gather_gradients(mine, arrived, (forward_rows, inverse_parts), place)
-    forward_pair, *sends = forward_messages(entries, live_tiles, forward_rows, weights)
+    held = forward_messages(entries, live_tiles, forward_rows, weights)
+    gathered, (forward_pair, *sends, inverse_parts) = gather_gradients(mine, arrived, (*held, inverse_parts), place)
     sends = [from_column(part, dy=Y - dy) for dy, part in enumerate(sends, 1)]
     base = relations // LANES * LANES
     window = -(-(2 * relations - base) // LANES) * LANES

time: 123 us -> 125 us (1.016); the launches traced: 123 us -> 122 us
  waiting for transfers between devices: 34.6 us -> 31.9 us
  starting transfers between devices: 46.9 us -> 49.3 us
    ppermute x8, waiting for transfers between devices: 8.85 us -> 3.57 us  [from_column(): return lax.ppermute(array, 'pcol', pairs)]
    ppermute x8, starting transfers between devices: 9.38 us -> 14.2 us  [from_column(): return lax.ppermute(array, 'pcol', pairs)]
    all_to_all x1, waiting for transfers between devices: 4.56 us -> 8.2 us  [gather_gradients(): lax.all_to_all(copies, 'prow', 0, 0, tiled=True, axis_index_groups=row_gr...]
    all_to_all x1, starting transfers between devices: 8 us -> 5.69 us  [gather_gradients(): lax.all_to_all(copies, 'prow', 0, 0, tiled=True, axis_index_groups=row_gr...]
    ppermute x13, waiting for transfers between devices: 18 us -> 16.1 us  [from_row(): return lax.ppermute(array, 'prow', pairs)]
  transfers between devices with their start and end apart: 24 -> 24, of which waited for: 13 -> 8; matrix products, arithmetic and copies ran while one was open for 5% -> 5% of each run, Pallas kernels for 23% -> 24%
where the time goes in v2:
time: 125 us; the launch traced here: 122 us
  starting transfers between devices  49.3 us (39%)
  waiting for transfers between devices  31.9 us (26%)
  Pallas kernels  31.6 us (25%)
  other arithmetic  5.24 us (4%)
  local copies, waits for them, and re-layouts  1.9 us (2%)
  between operations  1.65 us (1%)
    ppermute x13, starting transfers between devices, from_row(): return lax.ppermute(array, 'prow', pairs)  17.1 us
    ppermute x13, waiting for transfers between devices, from_row(): return lax.ppermute(array, 'prow', pairs)  16.1 us
    ppermute x8, starting transfers between devices, from_column(): return lax.ppermute(array, 'pcol', pairs)  14.2 us
    pallas_call x1, Pallas kernels, gradients(): pl.pallas_call(functools.partial(gradient_kernel, len(columns), len(row_p...  9.03 us
    pallas_call x1, Pallas kernels, relation_weights(): pl.pallas_call(functools.partial(weights_kernel, parts), out_shape=jax.Sh...  8.34 us
    all_to_all x1, waiting for transfers between devices, gather_gradients(): lax.all_to_all(copies, 'prow', 0, 0, tiled=True, axis_index_groups=row_gr...  8.2 us
    all_to_all x1, starting transfers between devices, on_device(): lax.all_to_all(inverse_part, 'prow', 0, 0, tiled=True, axis_index_groups=...  6.9 us
    all_to_all x1, starting transfers between devices, gather_gradients(): lax.all_to_all(copies, 'prow', 0, 0, tiled=True, axis_index_groups=row_gr...  5.69 us
  transfers between devices with their start and end apart: 24, of which 8 were waited for; matrix products, arithmetic and copies ran while one was open for 5% of the time, Pallas kernels for 24%

profile of v2, /device:TPU:32, one launch (start us, length us, event | category | flops | bytes accessed | tf_op | source)
XLA Modules:
  0.0 122.3 jit_solution(10216142974114269466)
XLA Ops:
  0.7 2.0 %pack.1 = (bf16[1,256,256]{2,1,0:T(8,128)(2,1)}, bf16[8,256,256]{2,1,0:T(8,128)(2,1)}) custom-call(bf16[128,256]{1,0:T(8,128)(2,1)} %feature_ref.1, bf16[128,256]{1,0:T(8,128)(2,1)} %cotangent_ref.1), custom_call_target="tpu_custom_call" | custom-call | bytes 1000000 | tf_op jit(solution)/shard_map/pack/pallas_call | solution.py:396
  2.7 3.3 %collective-permute-start = (bf16[1,256,256]{2,1,0:T(8,128)(2,1)}, bf16[1,256,256]{2,1,0:T(8,128)(2,1)S(1)}, u32[]{:S(2)}, u32[]{:S(2)}) collective-permute-start(bf16[1,256,256]{2,1,0:T(8,128)(2,1)} %get-tuple-element.38.refs_1_), channel_id=1, source_target_pairs={{96,0},{104,8},{112,16},{120,24},{0,32},{8,40},{16,48},{24,56},{32... | collective-permute-start | bytes 393224 | tf_op jit(solution)/shard_map/ppermute | solution.py:419
  6.0 2.2 %collective-permute-start.1 = (bf16[1,256,256]{2,1,0:T(8,128)(2,1)}, bf16[1,256,256]{2,1,0:T(8,128)(2,1)S(1)}, u32[]{:S(2)}, u32[]{:S(2)}) collective-permute-start(bf16[1,256,256]{2,1,0:T(8,128)(2,1)} %get-tuple-element.38.refs_1_), channel_id=1, source_target_pairs={{32,0},{40,8},{48,16},{56,24},{64,32},{72,40},{80,48},{88,56},{96,... | collective-permute-start | bytes 393224 | tf_op jit(solution)/shard_map/ppermute | solution.py:419
  8.2 4.9 %collective-permute-start.2 = (bf16[1,256,256]{2,1,0:T(8,128)(2,1)}, bf16[1,256,256]{2,1,0:T(8,128)(2,1)S(1)}, u32[]{:S(2)}, u32[]{:S(2)}) collective-permute-start(bf16[1,256,256]{2,1,0:T(8,128)(2,1)} %get-tuple-element.38.refs_1_), channel_id=1, source_target_pairs={{64,0},{72,8},{80,16},{88,24},{96,32},{104,40},{112,48},{120,56},{... | collective-permute-start | bytes 393224 | tf_op jit(solution)/shard_map/ppermute | solution.py:419
  13.2 5.4 %all-to-all-start = ((bf16[8,256,256]{2,1,0:T(8,128)(2,1)}), bf16[8,256,256]{2,1,0:T(8,128)(2,1)S(1)}, u32[]{:S(2)}, u32[]{:S(2)}) async-start(bf16[8,256,256]{2,1,0:T(8,128)(2,1)} %get-tuple-element.40), calls=%async_computation | async-start | bytes 2097152 | tf_op jit(solution)/shard_map/all_to_all | solution.py:493
  18.7 5.5 %collective-permute-done.2.refs_3_ = bf16[1,256,256]{2,1,0:T(8,128)(2,1)S(1)} collective-permute-done((bf16[1,256,256]{2,1,0:T(8,128)(2,1)}, bf16[1,256,256]{2,1,0:T(8,128)(2,1)S(1)}, u32[]{:S(2)}, u32[]{:S(2)}) %collective-permute-start.2) | collective-permute-done | bytes 131104 | tf_op jit(solution)/shard_map/ppermute | solution.py:419
  24.9 3.1 %collective-permute-start.3 = (bf16[4,256,256]{2,1,0:T(8,128)(2,1)S(1)}, bf16[4,256,256]{2,1,0:T(8,128)(2,1)S(1)}, u32[]{:S(2)}, u32[]{:S(2)}) collective-permute-start(bf16[4,256,256]{2,1,0:T(8,128)(2,1)S(1)} %join.2.refs_0_), channel_id=1, source_target_pairs={{128,0},{136,8},{144,16},{152,24},{160,32},{168,40},{176,48},{184,... | collective-permute-start | bytes 1572872 | tf_op jit(solution)/shard_map/ppermute | solution.py:419
  29.3 8.3 %relation_weights.1.weights_ref = bf16[32,256,256]{2,1,0:T(8,128)(2,1)} custom-call(s32[1,32]{1,0:T(1,128)} %add_bitcast_fusion.row_ref, f32[32,2690]{1,0:T(8,128)} %bitcast.59, bf16[32,256,256]{2,1,0:T(8,128)(2,1)} %basis_ref.3), custom_call_target="tpu_custom_call" | custom-call | flops 4000000000 | bytes 8388608 | tf_op jit(solution)/shard_map/relation_weights/pallas_call | solution.py:74
  37.6 1.1 copy-done.4
  38.7 5.4 %inverse_messages.1 = (bf16[16,128,256]{2,1,0:T(8,128)(2,1)S(1)}, f32[2048,256]{1,0:T(8,128)}, bf16[2048,256]{1,0:T(8,128)(2,1)}) custom-call(s32[6,16]{1,0:T(8,128)S(1)} %stack.2.entry_ref, s32[1,1]{1,0:T(1,128)S(6)} %copy.10.live_ref, s32[16,128,128]{2,1,0:T(8,128)} %bitcast.56, bf16[32,256,256]{2,1,0:T(8,128)(2,1)} %relation_weights.1.weights_ref, ...), custom_call_target="tpu_custom_call" | custom-call | flops 1000000000 | bytes 8000000 | tf_op jit(solution)/shard_map/inverse_messages/pallas_call | solution.py:142
  45.4 1.8 %collective-permute-start.5 = (bf16[4,256,256]{2,1,0:T(8,128)(2,1)S(1)}, bf16[4,256,256]{2,1,0:T(8,128)(2,1)S(1)}, u32[]{:S(2)}, u32[]{:S(2)}) collective-permute-start(bf16[4,256,256]{2,1,0:T(8,128)(2,1)S(1)} %get-tuple-element.48), channel_id=1, source_target_pairs={{112,0},{120,8},{0,16},{8,24},{16,32},{24,40},{32,48},{40,56},{48,... | collective-permute-start | bytes 1572872 | tf_op jit(solution)/shard_map/ppermute | solution.py:419
  47.6 2.8 %add_convert_fusion = bf16[2048,256]{1,0:T(8,128)(2,1)} fusion(f32[2048,256]{1,0:T(8,128)} %get-tuple-element.49, bf16[2048,256]{1,0:T(8,128)(2,1)S(1)} %collective-permute-done.6), kind=kLoop, calls=%fused_computation.1 | loop fusion | flops 1572864 | bytes 4194304 | tf_op jit(solution)/shard_map/convert_element_type | solution.py:504
  50.4 8.9 %collective-permute-done.4.refs_2_ = bf16[4,256,256]{2,1,0:T(8,128)(2,1)S(1)} collective-permute-done((bf16[4,256,256]{2,1,0:T(8,128)(2,1)S(1)}, bf16[4,256,256]{2,1,0:T(8,128)(2,1)S(1)}, u32[]{:S(2)}, u32[]{:S(2)}) %collective-permute-start.4) | collective-permute-done | bytes 524320 | tf_op jit(solution)/shard_map/ppermute | solution.py:419
  59.9 6.9 %all-to-all-start.1 = ((bf16[16,128,256]{2,1,0:T(8,128)(2,1)}), bf16[16,128,256]{2,1,0:T(8,128)(2,1)}, u32[]{:S(2)}, u32[]{:S(2)}) async-start(bf16[16,128,256]{2,1,0:T(8,128)(2,1)} %bitcast.55), calls=%async_computation.1 | async-start | bytes 2097152 | tf_op jit(solution)/shard_map/all_to_all | solution.py:507
  66.8 9.0 %gradients.1 = (bf16[16,128,256]{2,1,0:T(8,128)(2,1)}, bf16[48,16]{1,0:T(8,128)(2,1)S(1)}, bf16[48,16]{1,0:T(8,128)(2,1)S(1)}) custom-call(s32[6,16]{1,0:T(8,128)S(1)} %stack.2.entry_ref, s32[1,1]{1,0:T(1,128)S(6)} %copy.10.live_ref, s32[1]{0:T(128)} %bitcast.3.core_ref, s32[16,128,128]{2,1,0:T(8,128)} %bitcast.57, bf16[16,128,256]{2,1,0:T(8,128)(2,1)} %copy-done.3, ...), custom_call_target="tpu_custom_call" | custom-call | flops 4000000000 | bytes 12000000 | tf_op jit(solution)/shard_map/gradients/pallas_call | solution.py:265
  75.9 1.2 collective-permute-done.11
  77.2 1.0 collective-permute-start.12
  78.2 2.8 %collective-permute-done.12 = bf16[48,32]{1,0:T(8,128)(2,1)S(1)} collective-permute-done((bf16[48,32]{1,0:T(8,128)(2,1)S(1)}, bf16[48,32]{1,0:T(8,128)(2,1)S(1)}, u32[]{:S(2)}, u32[]{:S(2)}) %collective-permute-start.12) | collective-permute-done | bytes 3104 | tf_op jit(solution)/shard_map/ppermute | solution.py:427
  81.1 1.1 collective-permute-start.13
  82.2 2.7 %collective-permute-start.14 = (bf16[48,64]{1,0:T(8,128)(2,1)S(1)}, bf16[48,64]{1,0:T(8,128)(2,1)S(1)}, u32[]{:S(2)}, u32[]{:S(2)}) collective-permute-start(bf16[48,64]{1,0:T(8,128)(2,1)S(1)} %pad_maximum_fusion.2), channel_id=1, source_target_pairs={{4,0},{5,1},{6,2},{7,3},{0,4},{1,5},{2,6},{3,7},{12,8},{13,9},{14,... | collective-permute-start | bytes 18440 | tf_op jit(solution)/shard_map/ppermute | solution.py:427
  84.9 1.4 %collective-permute-start.15 = (bf16[48,64]{1,0:T(8,128)(2,1)S(1)}, bf16[48,64]{1,0:T(8,128)(2,1)S(1)}, u32[]{:S(2)}, u32[]{:S(2)}) collective-permute-start(bf16[48,64]{1,0:T(8,128)(2,1)S(1)} %pad_maximum_fusion.2), channel_id=1, source_target_pairs={{2,0},{3,1},{4,2},{5,3},{6,4},{7,5},{0,6},{1,7},{10,8},{11,9},{12,... | collective-permute-start | bytes 18440 | tf_op jit(solution)/shard_map/ppermute | solution.py:427
  86.3 4.2 %forward_messages.1 = (f32[2,128,256]{2,1,0:T(8,128)}, bf16[2,128,256]{2,1,0:T(8,128)(2,1)}, bf16[2,128,256]{2,1,0:T(8,128)(2,1)}, bf16[2,128,256]{2,1,0:T(8,128)(2,1)}) custom-call(s32[6,16]{1,0:T(8,128)} %copy-done.2, s32[1,1]{1,0:T(1,128)S(6)} %copy.10.live_ref, bf16[16,128,256]{2,1,0:T(8,128)(2,1)} %get-tuple-element.59.rows_ref, ...), custom_call_target="tpu_custom_call" | custom-call | flops 1000000000 | bytes 4000000 | tf_op jit(solution)/shard_map/forward_messages/pallas_call | solution.py:184
  90.6 4.1 %all-to-all-done.1 = bf16[16,128,256]{2,1,0:T(8,128)(2,1)} async-done(((bf16[16,128,256]{2,1,0:T(8,128)(2,1)}), bf16[16,128,256]{2,1,0:T(8,128)(2,1)}, u32[]{:S(2)}, u32[]{:S(2)}) %all-to-all-start.1) | async-done | bytes 1048608 | tf_op jit(solution)/shard_map/all_to_all | solution.py:507
  95.5 5.7 %all-to-all-start.2 = ((bf16[16,48,256]{2,1,0:T(8,128)(2,1)}), bf16[16,48,256]{2,1,0:T(8,128)(2,1)S(1)}, u32[]{:S(2)}, u32[]{:S(2)}) async-start(bf16[16,48,256]{2,1,0:T(8,128)(2,1)} %broadcast_in_dim.10), calls=%async_computation.2 | async-start | bytes 786432 | tf_op jit(solution)/shard_map/all_to_all | solution.py:472
  101.2 0.9 collective-permute-start.16
  102.1 2.6 %collective-permute-start.17 = (bf16[2,128,256]{2,1,0:T(8,128)(2,1)}, bf16[2,128,256]{2,1,0:T(8,128)(2,1)S(1)}, u32[]{:S(2)}, u32[]{:S(2)}) collective-permute-start(bf16[2,128,256]{2,1,0:T(8,128)(2,1)} %get-tuple-element.69), channel_id=1, source_target_pairs={{4,0},{5,1},{6,2},{7,3},{0,4},{1,5},{2,6},{3,7},{12,8},{13,9},{14,... | collective-permute-start | bytes 393224 | tf_op jit(solution)/shard_map/ppermute | solution.py:427
  104.7 2.1 %collective-permute-start.18 = (bf16[2,128,256]{2,1,0:T(8,128)(2,1)}, bf16[2,128,256]{2,1,0:T(8,128)(2,1)S(1)}, u32[]{:S(2)}, u32[]{:S(2)}) collective-permute-start(bf16[2,128,256]{2,1,0:T(8,128)(2,1)} %get-tuple-element.70), channel_id=1, source_target_pairs={{2,0},{3,1},{4,2},{5,3},{6,4},{7,5},{0,6},{1,7},{10,8},{11,9},{12,... | collective-permute-start | bytes 393224 | tf_op jit(solution)/shard_map/ppermute | solution.py:427
  106.8 8.2 %all-to-all-done.2.entry_ref = bf16[16,48,256]{2,1,0:T(8,128)(2,1)S(1)} async-done(((bf16[16,48,256]{2,1,0:T(8,128)(2,1)}), bf16[16,48,256]{2,1,0:T(8,128)(2,1)S(1)}, u32[]{:S(2)}, u32[]{:S(2)}) %all-to-all-start.2) | async-done | bytes 393248 | tf_op jit(solution)/shard_map/all_to_all | solution.py:472
  115.0 1.0 place_rows.1.own_ref
  116.1 2.4 %collective-permute-start.19 = (bf16[128,256]{1,0:T(8,128)(2,1)S(1)}, bf16[128,256]{1,0:T(8,128)(2,1)S(1)}, u32[]{:S(2)}, u32[]{:S(2)}) collective-permute-start(bf16[128,256]{1,0:T(8,128)(2,1)S(1)} %fusion.4), channel_id=1, source_target_pairs={{1,0},{0,1},{3,2},{2,3},{5,4},{4,5},{7,6},{6,7},{9,8},{8,9},{11,10... | collective-permute-start | bytes 196616 | tf_op jit(solution)/shard_map/ppermute | solution.py:427
  118.5 1.4 %convert_reduce_fusion = f32[128,256]{1,0:T(8,128)S(1)} fusion(bf16[16,128,256]{2,1,0:T(8,128)(2,1)} %all-to-all-done.1), kind=kLoop, calls=%fused_computation | loop fusion | flops 1015808 | bytes 1179648 | tf_op jit(solution)/shard_map/reduce_sum | solution.py:524
  120.8 0.8 fusion.3
  (60 shorter events, 6.6 us)
Async XLA Ops:
  0.6 120.1 %copy-start = (bf16[256,256]{1,0:T(8,128)(2,1)S(1)}, bf16[256,256]{1,0:T(8,128)(2,1)}, u32[]{:S(2)}) copy-start(bf16[256,256]{1,0:T(8,128)(2,1)} %param.10) | copy-start | bytes 393220
  0.6 17.9 %copy-start.7 = (s32[1,1,16,3]{2,1,3,0:T(1,128)S(1)}, s32[1,1,16,3]{2,1,3,0:T(1,128)}, u32[]{:S(2)}) copy-start(s32[1,1,16,3]{2,1,3,0:T(1,128)} %param.13) | copy-start | bytes 580
  2.7 21.5 %copy-start.1 = (bf16[1,256,256]{2,1,0:T(8,128)(2,1)S(1)}, bf16[1,256,256]{2,1,0:T(8,128)(2,1)}, u32[]{:S(2)}) copy-start(bf16[1,256,256]{2,1,0:T(8,128)(2,1)} %get-tuple-element.38.refs_1_) | copy-start | bytes 393220
  2.7 16.0 %collective-permute-start = (bf16[1,256,256]{2,1,0:T(8,128)(2,1)}, bf16[1,256,256]{2,1,0:T(8,128)(2,1)S(1)}, u32[]{:S(2)}, u32[]{:S(2)}) collective-permute-start(bf16[1,256,256]{2,1,0:T(8,128)(2,1)} %get-tuple-element.38.refs_1_), channel_id=1, source_target_pairs={{96,0},{104,8},{112,16},{120,24},{0,32},{8,40},{16,48},{24,56},{32... | collective-permute-start | bytes 393224 | tf_op jit(solution)/shard_map/ppermute | solution.py:419
  6.0 12.7 %collective-permute-start.1 = (bf16[1,256,256]{2,1,0:T(8,128)(2,1)}, bf16[1,256,256]{2,1,0:T(8,128)(2,1)S(1)}, u32[]{:S(2)}, u32[]{:S(2)}) collective-permute-start(bf16[1,256,256]{2,1,0:T(8,128)(2,1)} %get-tuple-element.38.refs_1_), channel_id=1, source_target_pairs={{32,0},{40,8},{48,16},{56,24},{64,32},{72,40},{80,48},{88,56},{96,... | collective-permute-start | bytes 393224 | tf_op jit(solution)/shard_map/ppermute | solution.py:419
  8.2 15.9 %collective-permute-start.2 = (bf16[1,256,256]{2,1,0:T(8,128)(2,1)}, bf16[1,256,256]{2,1,0:T(8,128)(2,1)S(1)}, u32[]{:S(2)}, u32[]{:S(2)}) collective-permute-start(bf16[1,256,256]{2,1,0:T(8,128)(2,1)} %get-tuple-element.38.refs_1_), channel_id=1, source_target_pairs={{64,0},{72,8},{80,16},{88,24},{96,32},{104,40},{112,48},{120,56},{... | collective-permute-start | bytes 393224 | tf_op jit(solution)/shard_map/ppermute | solution.py:419
  13.2 24.5 %all-to-all-start = ((bf16[8,256,256]{2,1,0:T(8,128)(2,1)}), bf16[8,256,256]{2,1,0:T(8,128)(2,1)S(1)}, u32[]{:S(2)}, u32[]{:S(2)}) async-start(bf16[8,256,256]{2,1,0:T(8,128)(2,1)} %get-tuple-element.40), calls=%async_computation | async-start | bytes 2097152 | tf_op jit(solution)/shard_map/all_to_all | solution.py:493
  24.9 19.3 %collective-permute-start.3 = (bf16[4,256,256]{2,1,0:T(8,128)(2,1)S(1)}, bf16[4,256,256]{2,1,0:T(8,128)(2,1)S(1)}, u32[]{:S(2)}, u32[]{:S(2)}) collective-permute-start(bf16[4,256,256]{2,1,0:T(8,128)(2,1)S(1)} %join.2.refs_0_), channel_id=1, source_target_pairs={{128,0},{136,8},{144,16},{152,24},{160,32},{168,40},{176,48},{184,... | collective-permute-start | bytes 1572872 | tf_op jit(solution)/shard_map/ppermute | solution.py:419
  29.3 37.5 %copy-start.2 = (s32[6,16]{1,0:T(8,128)}, s32[6,16]{1,0:T(8,128)S(1)}, u32[]{:S(2)}) copy-start(s32[6,16]{1,0:T(8,128)S(1)} %stack.2.entry_ref) | copy-start | bytes 1156
  37.6 1.1 copy-start.4
  44.2 6.3 %copy-start.3 = (bf16[16,128,256]{2,1,0:T(8,128)(2,1)}, bf16[16,128,256]{2,1,0:T(8,128)(2,1)S(1)}, u32[]{:S(2)}) copy-start(bf16[16,128,256]{2,1,0:T(8,128)(2,1)S(1)} %get-tuple-element.44.inverse_ref) | copy-start | bytes 3145732
  44.2 3.5 %collective-permute-start.6 = (bf16[2048,256]{1,0:T(8,128)(2,1)}, bf16[2048,256]{1,0:T(8,128)(2,1)S(1)}, u32[]{:S(2)}, u32[]{:S(2)}) collective-permute-start(bf16[2048,256]{1,0:T(8,128)(2,1)} %get-tuple-element.50), channel_id=1, source_target_pairs={{8,0},{0,8},{24,16},{16,24},{40,32},{32,40},{56,48},{48,56},{72,64... | collective-permute-start | bytes 3145736 | tf_op jit(solution)/shard_map/ppermute | solution.py:419
  44.3 6.2 %collective-permute-start.7 = (bf16[4,256,256]{2,1,0:T(8,128)(2,1)S(1)}, bf16[4,256,256]{2,1,0:T(8,128)(2,1)S(1)}, u32[]{:S(2)}, u32[]{:S(2)}) collective-permute-start(bf16[4,256,256]{2,1,0:T(8,128)(2,1)S(1)} %join.2.refs_0_), channel_id=1, source_target_pairs={{8,0},{0,8},{24,16},{16,24},{40,32},{32,40},{56,48},{48,56},{72,64... | collective-permute-start | bytes 1572872 | tf_op jit(solution)/shard_map/ppermute | solution.py:419
  44.9 14.5 %collective-permute-start.8 = (bf16[4,256,256]{2,1,0:T(8,128)(2,1)S(1)}, bf16[4,256,256]{2,1,0:T(8,128)(2,1)S(1)}, u32[]{:S(2)}, u32[]{:S(2)}) collective-permute-start(bf16[4,256,256]{2,1,0:T(8,128)(2,1)S(1)} %collective-permute-done.3.refs_1_), channel_id=1, source_target_pairs={{8,0},{0,8},{24,16},{16,24},{40,32},{32,40},{56,48},{48,56},{72,64... | collective-permute-start | bytes 1572872 | tf_op jit(solution)/shard_map/ppermute | solution.py:419
  45.1 14.3 %collective-permute-start.4 = (bf16[4,256,256]{2,1,0:T(8,128)(2,1)S(1)}, bf16[4,256,256]{2,1,0:T(8,128)(2,1)S(1)}, u32[]{:S(2)}, u32[]{:S(2)}) collective-permute-start(bf16[4,256,256]{2,1,0:T(8,128)(2,1)S(1)} %get-tuple-element.47), channel_id=1, source_target_pairs={{16,0},{24,8},{32,16},{40,24},{48,32},{56,40},{64,48},{72,56},{80,... | collective-permute-start | bytes 1572872 | tf_op jit(solution)/shard_map/ppermute | solution.py:419
  45.4 14.0 %collective-permute-start.5 = (bf16[4,256,256]{2,1,0:T(8,128)(2,1)S(1)}, bf16[4,256,256]{2,1,0:T(8,128)(2,1)S(1)}, u32[]{:S(2)}, u32[]{:S(2)}) collective-permute-start(bf16[4,256,256]{2,1,0:T(8,128)(2,1)S(1)} %get-tuple-element.48), channel_id=1, source_target_pairs={{112,0},{120,8},{0,16},{8,24},{16,32},{24,40},{32,48},{40,56},{48,... | collective-permute-start | bytes 1572872 | tf_op jit(solution)/shard_map/ppermute | solution.py:419
  59.3 7.4 %collective-permute-start.10 = (bf16[4,256,256]{2,1,0:T(8,128)(2,1)S(1)}, bf16[4,256,256]{2,1,0:T(8,128)(2,1)}, u32[]{:S(2)}, u32[]{:S(2)}) collective-permute-start(bf16[4,256,256]{2,1,0:T(8,128)(2,1)S(1)} %collective-permute-done.5.refs_3_), channel_id=1, source_target_pairs={{8,0},{0,8},{24,16},{16,24},{40,32},{32,40},{56,48},{48,56},{72,64... | collective-permute-start | bytes 1572872 | tf_op jit(solution)/shard_map/ppermute | solution.py:419
  59.4 7.4 %collective-permute-start.9 = (bf16[4,256,256]{2,1,0:T(8,128)(2,1)S(1)}, bf16[4,256,256]{2,1,0:T(8,128)(2,1)}, u32[]{:S(2)}, u32[]{:S(2)}) collective-permute-start(bf16[4,256,256]{2,1,0:T(8,128)(2,1)S(1)} %collective-permute-done.4.refs_2_), channel_id=1, source_target_pairs={{8,0},{0,8},{24,16},{16,24},{40,32},{32,40},{56,48},{48,56},{72,64... | collective-permute-start | bytes 1572872 | tf_op jit(solution)/shard_map/ppermute | solution.py:419
  59.9 34.9 %all-to-all-start.1 = ((bf16[16,128,256]{2,1,0:T(8,128)(2,1)}), bf16[16,128,256]{2,1,0:T(8,128)(2,1)}, u32[]{:S(2)}, u32[]{:S(2)}) async-start(bf16[16,128,256]{2,1,0:T(8,128)(2,1)} %bitcast.55), calls=%async_computation.1 | async-start | bytes 2097152 | tf_op jit(solution)/shard_map/all_to_all | solution.py:507
  75.8 1.3 %collective-permute-start.11 = (bf16[48,16]{1,0:T(8,128)(2,1)S(1)}, bf16[48,16]{1,0:T(8,128)(2,1)S(1)}, u32[]{:S(2)}, u32[]{:S(2)}) collective-permute-start(bf16[48,16]{1,0:T(8,128)(2,1)S(1)} %get-tuple-element.56), channel_id=1, source_target_pairs={{8,0},{0,8},{24,16},{16,24},{40,32},{32,40},{56,48},{48,56},{72,64... | collective-permute-start | bytes 4616 | tf_op jit(solution)/shard_map/ppermute | solution.py:419
  77.2 3.8 %collective-permute-start.12 = (bf16[48,32]{1,0:T(8,128)(2,1)S(1)}, bf16[48,32]{1,0:T(8,128)(2,1)S(1)}, u32[]{:S(2)}, u32[]{:S(2)}) collective-permute-start(bf16[48,32]{1,0:T(8,128)(2,1)S(1)} %pad_maximum_fusion.1), channel_id=1, source_target_pairs={{1,0},{0,1},{3,2},{2,3},{5,4},{4,5},{7,6},{6,7},{9,8},{8,9},{11,10... | collective-permute-start | bytes 9224 | tf_op jit(solution)/shard_map/ppermute | solution.py:427
  81.1 9.4 %collective-permute-start.13 = (bf16[48,64]{1,0:T(8,128)(2,1)S(1)}, bf16[48,64]{1,0:T(8,128)(2,1)S(1)}, u32[]{:S(2)}, u32[]{:S(2)}) collective-permute-start(bf16[48,64]{1,0:T(8,128)(2,1)S(1)} %pad_maximum_fusion.2), channel_id=1, source_target_pairs={{6,0},{7,1},{0,2},{1,3},{2,4},{3,5},{4,6},{5,7},{14,8},{15,9},{8,1... | collective-permute-start | bytes 18440 | tf_op jit(solution)/shard_map/ppermute | solution.py:427
  82.2 8.3 %collective-permute-start.14 = (bf16[48,64]{1,0:T(8,128)(2,1)S(1)}, bf16[48,64]{1,0:T(8,128)(2,1)S(1)}, u32[]{:S(2)}, u32[]{:S(2)}) collective-permute-start(bf16[48,64]{1,0:T(8,128)(2,1)S(1)} %pad_maximum_fusion.2), channel_id=1, source_target_pairs={{4,0},{5,1},{6,2},{7,3},{0,4},{1,5},{2,6},{3,7},{12,8},{13,9},{14,... | collective-permute-start | bytes 18440 | tf_op jit(solution)/shard_map/ppermute | solution.py:427
  84.9 5.6 %collective-permute-start.15 = (bf16[48,64]{1,0:T(8,128)(2,1)S(1)}, bf16[48,64]{1,0:T(8,128)(2,1)S(1)}, u32[]{:S(2)}, u32[]{:S(2)}) collective-permute-start(bf16[48,64]{1,0:T(8,128)(2,1)S(1)} %pad_maximum_fusion.2), channel_id=1, source_target_pairs={{2,0},{3,1},{4,2},{5,3},{6,4},{7,5},{0,6},{1,7},{10,8},{11,9},{12,... | collective-permute-start | bytes 18440 | tf_op jit(solution)/shard_map/ppermute | solution.py:427
  95.5 20.5 %copy-start.5 = (f32[2,128,256]{2,1,0:T(8,128)S(1)}, f32[2,128,256]{2,1,0:T(8,128)}, u32[]{:S(2)}) copy-start(f32[2,128,256]{2,1,0:T(8,128)} %get-tuple-element.66) | copy-start | bytes 786436
  95.5 19.5 %all-to-all-start.2 = ((bf16[16,48,256]{2,1,0:T(8,128)(2,1)}), bf16[16,48,256]{2,1,0:T(8,128)(2,1)S(1)}, u32[]{:S(2)}, u32[]{:S(2)}) async-start(bf16[16,48,256]{2,1,0:T(8,128)(2,1)} %broadcast_in_dim.10), calls=%async_computation.2 | async-start | bytes 786432 | tf_op jit(solution)/shard_map/all_to_all | solution.py:472
  101.2 19.6 %copy-start.6 = (bf16[128,256]{1,0:T(8,128)(2,1)S(1)}, bf16[128,256]{1,0:T(8,128)(2,1)}, u32[]{:S(2)}) copy-start(bf16[128,256]{1,0:T(8,128)(2,1)} %feature_ref.1) | copy-start | bytes 196612
  101.2 14.8 %collective-permute-start.16 = (bf16[2,128,256]{2,1,0:T(8,128)(2,1)}, bf16[2,128,256]{2,1,0:T(8,128)(2,1)S(1)}, u32[]{:S(2)}, u32[]{:S(2)}) collective-permute-start(bf16[2,128,256]{2,1,0:T(8,128)(2,1)} %get-tuple-element.68), channel_id=1, source_target_pairs={{6,0},{7,1},{0,2},{1,3},{2,4},{3,5},{4,6},{5,7},{14,8},{15,9},{8,1... | collective-permute-start | bytes 393224 | tf_op jit(solution)/shard_map/ppermute | solution.py:427
  102.1 13.9 %collective-permute-start.17 = (bf16[2,128,256]{2,1,0:T(8,128)(2,1)}, bf16[2,128,256]{2,1,0:T(8,128)(2,1)S(1)}, u32[]{:S(2)}, u32[]{:S(2)}) collective-permute-start(bf16[2,128,256]{2,1,0:T(8,128)(2,1)} %get-tuple-element.69), channel_id=1, source_target_pairs={{4,0},{5,1},{6,2},{7,3},{0,4},{1,5},{2,6},{3,7},{12,8},{13,9},{14,... | collective-permute-start | bytes 393224 | tf_op jit(solution)/shard_map/ppermute | solution.py:427
  104.7 11.3 %collective-permute-start.18 = (bf16[2,128,256]{2,1,0:T(8,128)(2,1)}, bf16[2,128,256]{2,1,0:T(8,128)(2,1)S(1)}, u32[]{:S(2)}, u32[]{:S(2)}) collective-permute-start(bf16[2,128,256]{2,1,0:T(8,128)(2,1)} %get-tuple-element.70), channel_id=1, source_target_pairs={{2,0},{3,1},{4,2},{5,3},{6,4},{7,5},{0,6},{1,7},{10,8},{11,9},{12,... | collective-permute-start | bytes 393224 | tf_op jit(solution)/shard_map/ppermute | solution.py:427
  116.1 4.6 %collective-permute-start.19 = (bf16[128,256]{1,0:T(8,128)(2,1)S(1)}, bf16[128,256]{1,0:T(8,128)(2,1)S(1)}, u32[]{:S(2)}, u32[]{:S(2)}) collective-permute-start(bf16[128,256]{1,0:T(8,128)(2,1)S(1)} %fusion.4), channel_id=1, source_target_pairs={{1,0},{0,1},{3,2},{2,3},{5,4},{4,5},{7,6},{6,7},{9,8},{8,9},{11,10... | collective-permute-start | bytes 196616 | tf_op jit(solution)/shard_map/ppermute | solution.py:427
  119.9 1.7 %collective-permute-start.20 = (f32[32,1536]{1,0:T(8,128)S(1)}, f32[32,1536]{1,0:T(8,128)S(1)}, u32[]{:S(2)}, u32[]{:S(2)}) collective-permute-start(f32[32,1536]{1,0:T(8,128)S(1)} %place_rows.1.own_ref), channel_id=1, source_target_pairs={{8,0},{0,8},{24,16},{16,24},{40,32},{32,40},{56,48},{48,56},{72,64... | collective-permute-start | bytes 589832 | tf_op jit(solution)/shard_map/ppermute | solution.py:419
